TPU v7x, 128 devices: a whole 4x4x4 slice. The times are simulated.
128 devices in a mesh: img: 8 (over x, z_lo), txt: 16 (over y, z_hi, core).
Axes of the slice: x: 4, y: 4, z: 4 (z_hi: 2, z_lo: 2; z = z_hi * 2 + z_lo), core: 2. Of those that a mesh axis runs over, the one named last changes fastest.
Arguments:
- image: bfloat16 [20480, 1152], P(('img', 'txt')), may hold values from -6 to 6
- text: bfloat16 [20480, 1152], P('txt', 'img'), may hold values from -6 to 6
- pair_text: int32 [20480], P(('img', 'txt')), may hold values from 0 to 20479, each once
- log_scale: float32 [1], replicated, may hold values from 2.3 to 3
- bias: float32 [1], replicated, may hold values from -3 to -1
Outputs:
- grad_image: bfloat16 [20480, 1152], P(('img', 'txt'))
- grad_text: bfloat16 [20480, 1152], P('txt', 'img')
Inputs may be any that keep to these rules, and one draw needn't show every extreme that they name: `pair_text`: each text index is the match of exactly one image.
All inputs are finite; a program needn't handle non-finite values.
Results may differ from a plain program's by a relative error of at most 0.0034.
Values may be sent and summed in bfloat16 or wider, within the bound.
No kernel may reach another device: no remote copies, remote signals or barrier semaphores. Data moves between devices by JAX's collectives and lax.ppermute only.
A program may use at most 128 MiB of HBM per device.

v0:
```python
import jax
import jax.numpy as jnp
from jax import lax
from jax.experimental import pallas as pl
from jax.experimental.pallas import tpu as pltpu
from jax.sharding import PartitionSpec as P

F32 = jnp.float32
BF16 = jnp.bfloat16
VMEM = pl.BlockSpec(memory_space=pltpu.VMEM)
SMEM = pl.BlockSpec(memory_space=pltpu.SMEM)
LOG2E = 1.4426950408889634
AXES = ("img", "txt")
NN = (((1,), (0,)), ((), ()))
NT = (((1,), (1,)), ((), ()))
TN = (((0,), (0,)), ((), ()))
STEPS = (0, -1, 1, 2)
TAIL = 16


def params(mib):
    return pltpu.CompilerParams(vmem_limit_bytes=mib * 2**20)


def cost(flops, size):
    return pl.CostEstimate(flops=flops, bytes_accessed=size, transcendentals=0)


def moves():
    def perm(f):
        pairs = []
        for x in range(4):
            for y in range(4):
                for hi in range(2):
                    for lo in range(2):
                        for c in range(2):
                            a = (x, y, hi, lo, c)
                            number = lambda x, y, hi, lo, c: (x * 2 + lo) * 16 + (y * 2 + hi) * 2 + c
                            pairs.append((number(*a), number(*f(*a))))
        return pairs

    out = {}
    for s in (1, -1, 2):
        out["y", s] = perm(lambda x, y, hi, lo, c: (x, (y + s) % 4, hi, lo, c))
        out["x", s] = perm(lambda x, y, hi, lo, c: ((x + s) % 4, y, hi, lo, c))
    out["hi"] = perm(lambda x, y, hi, lo, c: (x, y, 1 - hi, lo, c))
    out["lo"] = perm(lambda x, y, hi, lo, c: (x, y, hi, 1 - lo, c))
    out["core"] = perm(lambda x, y, hi, lo, c: (x, y, hi, lo, 1 - c))
    return out


MOVES = moves()


def send(value, move):
    return lax.ppermute(value, AXES, MOVES[move])


def after(value, *others):
    return lax.optimization_barrier((value, *others))[0]


def split3(value, rounded=lambda v: v.astype(BF16).astype(F32)):
    high = rounded(value)
    middle = rounded(value - high)
    return high, middle, rounded(value - high - middle)


def unit_kernel(image, pairs, out, inverse):
    value = image[...].astype(F32)
    scale = 1.0 / jnp.sqrt(jnp.sum(value * value, axis=1, keepdims=True) + 1e-06)
    inverse[...] = scale
    unit = (value * scale).astype(BF16)
    rows, width = unit.shape
    half = rows // 2
    out[:half, :] = unit[:half]
    out[half + TAIL :, :] = unit[half:]
    index = pairs[...]
    kind = lax.broadcasted_iota(jnp.int32, (TAIL, rows), 0)
    part = jnp.where(kind == 0, index >> 8, jnp.where(kind == 1, index & 255, 0))
    out[half : half + TAIL, :] = jnp.zeros((TAIL, width), BF16)
    out[half : half + TAIL, :rows] = part.astype(F32).astype(BF16)


def image_units(image, pairs):
    rows, width = image.shape
    pairs = pairs[None]
    return pl.pallas_call(
        unit_kernel,
        out_shape=[
            jax.ShapeDtypeStruct((rows + TAIL, width), BF16),
            jax.ShapeDtypeStruct((rows, 1), F32),
        ],
        in_specs=[VMEM] * 2,
        out_specs=[VMEM] * 2,
        compiler_params=params(8),
        cost_estimate=cost(0, 4 * rows * width),
        name="image_units",
    )(image, pairs)


def text_kernel(place, *refs):
    pieces, (unit, raw, inverse) = refs[:-3], refs[-3:]
    total = None
    for piece in pieces:
        value = piece[...].astype(F32)
        part = jnp.sum(value * value, axis=0, keepdims=True)
        total = part if total is None else total + part
    scale = 1.0 / jnp.sqrt(total + 1e-06)
    inverse[...] = scale
    depth = unit.shape[0] // 8
    block = 0
    for piece in pieces:
        for start in range(0, piece.shape[0], depth):
            rows = pl.ds(pl.multiple_of(place[block] * depth, 16), depth)
            value = piece[start : start + depth, :]
            raw[rows, :] = value
            unit[rows, :] = (value.astype(F32) * scale).astype(BF16)
            block += 1


def text_units(place, pieces, depth):
    width = pieces[0].shape[1]
    whole = jax.ShapeDtypeStruct((8 * depth, width), BF16)
    return pl.pallas_call(
        text_kernel,
        out_shape=[whole, whole, jax.ShapeDtypeStruct((1, width), F32)],
        in_specs=[SMEM] + [VMEM] * len(pieces),
        out_specs=[VMEM] * 3,
        compiler_params=params(12),
        cost_estimate=cost(40_000_000_000, 32 * depth * width),
        name="text_units",
    )(place, *pieces)


def weight_kernel(rows, scalars, first_text, *refs):
    pieces, text, (image, weight, other, tails) = refs[:-5], refs[-5], refs[-4:]
    half = rows // 2
    halves = []
    for piece in pieces:
        done = 0
        while done < piece.shape[0]:
            halves.append((piece, done))
            done += half + TAIL if len(halves) % 2 else half
    for block in range(8):
        (a, i), (b, j) = halves[2 * block : 2 * block + 2]
        at = block * rows
        image[at : at + half, :] = a[i : i + half, :]
        image[at + half : at + rows, :] = b[j : j + half, :]
        tails[block * TAIL : (block + 1) * TAIL, :] = a[i + half : i + half + TAIL, :rows]
    slope, shift = scalars[0], scalars[1]
    columns = text.shape[1]
    eye = lax.broadcasted_iota(jnp.int32, (rows, rows), 0) == lax.broadcasted_iota(
        jnp.int32, (rows, rows), 1
    )
    names = (lax.broadcasted_iota(jnp.int32, (rows, columns), 1) + first_text[0]).astype(F32)

    def step(number, carry):
        for k in range(4):
            block = number * 4 + k
            mine = pl.ds(pl.multiple_of(block * rows, 16), rows)
            tail = tails[pl.ds(pl.multiple_of(block * TAIL, 16), TAIL), :].astype(F32)
            product = lax.dot_general(
                image[mine, :], text[...], NN, preferred_element_type=F32
            )
            chance = 1.0 / (1.0 + jnp.exp2(product * slope + shift))
            match = jnp.sum(
                jnp.where(eye, tail[0:1] * 256.0 + tail[1:2], 0.0), axis=1, keepdims=True
            )
            weight[mine, :] = (chance - jnp.where(match == names, 1.0, 0.0)).astype(BF16)
        return carry

    lax.fori_loop(0, 8 // 4, step, 0)
    other[...] = weight[4 * rows :, :]


def weights(scalars, first_text, pieces, rows, text):
    width, columns = text.shape
    count = 8 * rows
    return pl.pallas_call(
        lambda *refs: weight_kernel(rows, *refs),
        out_shape=[
            jax.ShapeDtypeStruct((count, width), BF16),
            jax.ShapeDtypeStruct((count, columns), BF16),
            jax.ShapeDtypeStruct((count // 2, columns), BF16),
        ],
        in_specs=[SMEM, SMEM] + [VMEM] * (len(pieces) + 1),
        out_specs=[VMEM] * 3,
        scratch_shapes=[pltpu.VMEM((8 * TAIL, rows), BF16)],
        compiler_params=params(12),
        cost_estimate=cost(8_000_000_000, 2 * count * (width + columns)),
        name="weights",
    )(scalars, first_text, *pieces, text)


def text_back_kernel(place, image_a, weight_a, image_b, weight_b, raw, *refs):
    outs, back = refs[:8], refs[8]
    width, columns = back.shape
    block = 384
    dots = jnp.zeros((1, columns), F32)
    for f in range(0, width, block):
        part = lax.dot_general(
            image_a[:, f : f + block], weight_a[...], TN, preferred_element_type=F32
        ) + lax.dot_general(
            image_b[:, f : f + block], weight_b[...], TN, preferred_element_type=F32
        )
        back[f : f + block, :] = part
        dots += jnp.sum(part * raw[f : f + block, :].astype(F32), axis=0, keepdims=True)
    tail = split3(dots)
    empty = jnp.zeros((1, columns), F32)
    depth = width // 8
    for i in range(4):
        for h in range(2):
            out = outs[2 * i + h]
            start = pl.multiple_of(place[2 * i + h] * depth, 16)
            out[:depth, :] = back[pl.ds(start, depth), :].astype(out.dtype)
        spread = [empty] * 3 * i + list(tail) + [empty] * (TAIL - 3 * i - 3)
        out[depth:, :] = jnp.concatenate(spread, 0).astype(out.dtype)


def text_terms(place, image_a, weight_a, image_b, weight_b, raw):
    count, width = image_a.shape
    columns = weight_a.shape[1]
    return pl.pallas_call(
        text_back_kernel,
        out_shape=[
            jax.ShapeDtypeStruct((width // 8 + h * TAIL, columns), BF16 if i else F32)
            for i in range(4)
            for h in range(2)
        ],
        in_specs=[SMEM] + [VMEM] * 5,
        out_specs=[VMEM] * 8,
        scratch_shapes=[pltpu.VMEM((width, columns), F32)],
        compiler_params=params(16),
        cost_estimate=cost(4 * count * width * columns, 4 * count * columns),
        name="text_terms",
    )(place, image_a, weight_a, image_b, weight_b, raw)


def image_back_kernel(rows, own_a, got_a, own_b, got_b, text, text_got, *outs):
    for start in (2, 0):
        block = slice(start * rows, (start + 2) * rows)
        for h, (own, got) in enumerate(((own_a, got_a), (own_b, got_b))):
            back = lax.dot_general(
                own[block, :], text[...], NT, preferred_element_type=F32
            ) + lax.dot_general(got[block, :], text_got[...], NT, preferred_element_type=F32)
            for k in range(2):
                out = outs[2 * (start + k) + h]
                out[...] = back[k * rows : (k + 1) * rows].astype(out.dtype)


def image_terms(rows, own_a, got_a, own_b, got_b, text, text_got):
    width, columns = text.shape
    return pl.pallas_call(
        lambda *refs: image_back_kernel(rows, *refs),
        out_shape=[jax.ShapeDtypeStruct((rows, width), F32 if i < 2 else BF16) for i in range(8)],
        in_specs=[VMEM] * 6,
        out_specs=[VMEM] * 8,
        compiler_params=params(16),
        cost_estimate=cost(10_000_000_000, 8 * width * columns),
        name="image_terms",
    )(own_a, got_a, own_b, got_b, text, text_got)


def add_kernel(at, value, more, out):
    rows = more.shape[0]
    for start in range(0, value.shape[0], 16):
        block = slice(start, start + 16)
        if at <= start < at + rows:
            total = value[block, :].astype(F32) + more[start - at : start - at + 16, :].astype(F32)
            out[block, :] = total.astype(BF16)
        else:
            out[block, :] = value[block, :]


def add_rows(value, more, at):
    return pl.pallas_call(
        lambda *refs: add_kernel(at, *refs),
        out_shape=jax.ShapeDtypeStruct(value.shape, BF16),
        in_specs=[VMEM] * 2,
        out_specs=VMEM,
        compiler_params=params(8),
        cost_estimate=cost(5_000_000_000, 6 * value.size),
        name="add_rows",
    )(value, more)


def hold_kernel(value, *refs):
    refs[-1][...] = value[...]


def hold(value, *others):
    return pl.pallas_call(
        hold_kernel,
        out_shape=jax.ShapeDtypeStruct(value.shape, value.dtype),
        in_specs=[VMEM] + [pl.BlockSpec(memory_space=pl.ANY)] * len(others),
        out_specs=VMEM,
        compiler_params=params(4),
        cost_estimate=cost(20_000_000_000, 0),
        name="hold",
    )(value, *others)


def add_three_kernel(own, ahead, back, out):
    out[...] = (own[...] + ahead[...].astype(F32) + back[...].astype(F32)).astype(BF16)


def add_three(own, ahead, back):
    return pl.pallas_call(
        add_three_kernel,
        out_shape=jax.ShapeDtypeStruct(own.shape, BF16),
        in_specs=[VMEM] * 3,
        out_specs=VMEM,
        compiler_params=params(8),
        cost_estimate=cost(0, 10 * own.size),
        name="add_three",
    )(own, ahead, back)


def image_final_kernel(temper, own, ahead, back, given, image, inverse, out):
    total = own[...] + ahead[...].astype(F32) + back[...].astype(F32) + given[...].astype(F32)
    scale = inverse[...]
    unit = image[...].astype(F32) * scale
    dot = jnp.sum(unit * total, axis=1, keepdims=True)
    out[...] = (temper[0] * (total - unit * dot) * scale).astype(BF16)


def image_final(temper, own, ahead, back, given, image, inverse):
    return pl.pallas_call(
        image_final_kernel,
        out_shape=jax.ShapeDtypeStruct(image.shape, BF16),
        in_specs=[SMEM] + [VMEM] * 6,
        out_specs=VMEM,
        compiler_params=params(8),
        cost_estimate=cost(0, 16 * image.size),
        name="image_final",
    )(temper, own, ahead, back, given, image, inverse)


def text_final_kernel(temper, own, ahead, back, gave, given, raw, inverse, out):
    depth = raw.shape[0]
    scale = inverse[...]
    total = own[...] + ahead[...].astype(F32) + back[...].astype(F32)
    total += given[:depth, :].astype(F32)
    tails = gave[depth:, :].astype(F32) + given[depth:, :].astype(F32)
    dots = jnp.sum(tails, axis=0, keepdims=True) * scale
    unit = raw[...].astype(F32) * scale
    out[...] = (temper[0] * (total - unit * dots) * scale).astype(BF16)


def text_final(temper, own, ahead, back, gave, given, raw, inverse):
    return pl.pallas_call(
        text_final_kernel,
        out_shape=jax.ShapeDtypeStruct(raw.shape, BF16),
        in_specs=[SMEM] + [VMEM] * 7,
        out_specs=VMEM,
        compiler_params=params(8),
        cost_estimate=cost(0, 16 * raw.size),
        name="text_final",
    )(temper, own, ahead, back, gave, given, raw, inverse)


def local(image, text, pair_text, log_scale, bias):
    img, txt = lax.axis_index("img"), lax.axis_index("txt")
    x, lo = img // 2, img % 2
    place = jnp.stack([(x + s + 4) % 4 * 2 + (lo + h) % 2 for s in STEPS for h in range(2)])
    temper = jnp.exp(log_scale[0])
    scalars = jnp.stack([-LOG2E * temper, -LOG2E * bias[0]])
    first_text = (txt * text.shape[0])[None]
    depth, rows = text.shape[1], image.shape[0]

    own_text = text.T
    text_lo = send(own_text, "lo")
    text_a, text_b = send(own_text, ("x", 1)), send(own_text, ("x", -1))
    unit, image_inverse = image_units(image, pair_text)
    a, b = send(unit, ("y", 1)), send(unit, ("y", -1))
    unit_hi = send(hold(unit, text_lo), "hi")
    text_c, text_a = lax.optimization_barrier((text_lo, text_a))
    text_c = send(text_c, ("x", 1))
    text_d, text_b = lax.optimization_barrier((text_lo, text_b))
    text_d = send(text_d, ("x", -1))
    text_a2 = send(text_a, ("x", 1))
    cut = rows // 2 + TAIL
    a2, b2 = send(a[:cut], ("y", 1)), send(b[cut:], ("y", -1))
    c = send(unit_hi, ("y", 1))
    d, b = lax.optimization_barrier((unit_hi, b))
    d = send(d, ("y", -1))
    text_d2 = send(text_d, ("x", -1))
    c, d, text_c, text_d = lax.optimization_barrier((c, d, text_c, text_d))
    c2, d2 = send(c[:cut], ("y", 1)), send(d[cut:], ("y", -1))
    near, partner = [unit, a, b, a2, b2], [unit_hi, c, d, c2, d2]
    near.append(after(send(jnp.concatenate(near, 0), "core"), c2, d2))
    partner += [
        send(jnp.concatenate(partner[:3], 0), "core"),
        send(jnp.concatenate(partner[3:], 0), "core"),
    ]
    text_pieces = [own_text, text_lo, text_a, text_c, text_b, text_d, text_a2, text_d2]

    text_unit, text_raw, text_inverse = text_units(place, text_pieces, depth)
    image_a, weight_a, other_a = weights(scalars, first_text, near, rows, text_unit)
    got_a = send(other_a, "core")
    image_b, weight_b, other_b = weights(
        after(scalars, other_a), first_text, partner, rows, text_unit
    )
    got_b = send(other_b, "core")
    text_got = send(after(text_unit, other_b), "core")
    text_parts = text_terms(place, image_a, weight_a, image_b, weight_b, text_raw)
    got_b, *text_parts = lax.optimization_barrier((got_b, *text_parts))
    image_parts = image_terms(rows, weight_a, got_a, weight_b, got_b, text_unit, text_got)

    x_own, x_back, x_ahead, x_far = [text_parts[2 * i : 2 * i + 2] for i in range(4)]
    y_own, y_back, y_ahead, y_far = [image_parts[2 * i : 2 * i + 2] for i in range(4)]

    x_relay1, x_relay0 = send(x_far[1], ("x", -1)), send(x_far[0], ("x", 1))
    x_ahead1 = send(x_ahead[1], ("x", 1))
    y_relay1, y_relay0 = send(y_far[1], ("y", -1)), send(y_far[0], ("y", 1))
    x_back0, x_back1, x_ahead0, _ = lax.optimization_barrier((*x_back, x_ahead[0], y_own[0]))
    x_back1, x_ahead0 = add_rows(x_back1, x_relay1, 0), add_rows(x_ahead0, x_relay0, 0)
    x_ahead0, y_back0, y_back1, y_ahead0, y_ahead1 = lax.optimization_barrier(
        (x_ahead0, *y_back, *y_ahead)
    )
    x_back1, x_ahead0 = send(x_back1, ("x", -1)), send(x_ahead0, ("x", 1))
    y_back1 = add_rows(y_back1, y_relay1, 0)
    y_back1, y_ahead1, x_back0 = lax.optimization_barrier((y_back1, y_ahead1, x_back0))
    y_back1, y_ahead1 = send(y_back1, ("y", -1)), send(y_ahead1, ("y", 1))
    x_gave = add_three(x_own[1], x_ahead1, x_back1)
    x_given = send(x_gave, "lo")
    x_back0 = send(x_back0, ("x", -1))
    y_ahead0, y_back0 = lax.optimization_barrier((add_rows(y_ahead0, y_relay0, 0), y_back0))
    y_ahead0, y_back0 = send(y_ahead0, ("y", 1)), send(y_back0, ("y", -1))
    y_given = send(add_three(y_own[1], y_ahead1, y_back1), "hi")

    grad_text = text_final(
        temper[None], x_own[0], x_ahead0, x_back0, x_gave, x_given, own_text, text_inverse
    )
    y_given, grad_text = lax.optimization_barrier((y_given, grad_text))
    grad_image = image_final(
        temper[None], y_own[0], y_ahead0, y_back0, y_given, image, image_inverse
    )
    return grad_image, grad_text.T


def solution(mesh):
    in_specs = (P(("img", "txt"), None), P("txt", "img"), P(("img", "txt")), P(), P())
    out_specs = (P(("img", "txt"), None), P("txt", "img"))
    return jax.shard_map(local, mesh=mesh, in_specs=in_specs, out_specs=out_specs, check_vma=False)
```

profile of v0, /device:TPU:6, one launch (start us, length us, event | category | flops | bytes accessed | tf_op | source)
XLA Modules:
  0.0 116.4 jit_solution(13112113432192332882)
XLA Ops:
  0.6 2.0 %collective-permute-start.1 = (bf16[144,1280]{1,0:T(8,128)(2,1)}, bf16[144,1280]{1,0:T(8,128)(2,1)S(1)}, u32[]{:S(2)}, u32[]{:S(2)}) collective-permute-start(bf16[144,1280]{1,0:T(8,128)(2,1)} %bitcast.12), channel_id=1, source_target_pairs={{0,16},{1,17},{16,0},{17,1},{2,18},{3,19},{18,2},{19,3},{4,20},{5,... | collective-permute-start | bytes 1105928 | tf_op jit(solution)/shard_map/ppermute | solution.py:56
  3.5 2.4 %collective-permute-start.9 = (bf16[144,1280]{1,0:T(8,128)(2,1)}, bf16[144,1280]{1,0:T(8,128)(2,1)S(1)}, u32[]{:S(2)}, u32[]{:S(2)}) collective-permute-start(bf16[144,1280]{1,0:T(8,128)(2,1)} %bitcast.14), channel_id=1, source_target_pairs={{0,32},{1,33},{16,48},{17,49},{2,34},{3,35},{18,50},{19,51},{4,36}... | collective-permute-start | bytes 1105928 | tf_op jit(solution)/shard_map/ppermute | solution.py:56
  7.7 3.1 %collective-permute-start.3 = (bf16[176,1152]{1,0:T(8,128)(2,1)S(1)}, bf16[176,1152]{1,0:T(8,128)(2,1)S(1)}, u32[]{:S(2)}, u32[]{:S(2)}) collective-permute-start(bf16[176,1152]{1,0:T(8,128)(2,1)S(1)} %get-tuple-element.66.value.refs_2_), channel_id=1, source_target_pairs={{0,12},{1,13},{16,28},{17,29},{2,14},{3,15},{18,30},{19,31},{4,0},... | collective-permute-start | bytes 1216520 | tf_op jit(solution)/shard_map/ppermute | solution.py:56
  11.5 3.8 %collective-permute-start.2 = (bf16[176,1152]{1,0:T(8,128)(2,1)S(1)}, bf16[176,1152]{1,0:T(8,128)(2,1)S(1)}, u32[]{:S(2)}, u32[]{:S(2)}) collective-permute-start(bf16[176,1152]{1,0:T(8,128)(2,1)S(1)} %hold.1), channel_id=1, source_target_pairs={{0,2},{1,3},{16,18},{17,19},{2,0},{3,1},{18,16},{19,17},{4,6},{5,7... | collective-permute-start | bytes 1216520 | tf_op jit(solution)/shard_map/ppermute | solution.py:56
  18.0 1.5 %collective-permute-start.12 = (bf16[144,1280]{1,0:T(8,128)(2,1)S(1)}, bf16[144,1280]{1,0:T(8,128)(2,1)S(1)}, u32[]{:S(2)}, u32[]{:S(2)}) collective-permute-start(bf16[144,1280]{1,0:T(8,128)(2,1)S(1)} %collective-permute-done.1.refs_0_.refs_1_), channel_id=1, source_target_pairs={{0,96},{1,97},{16,112},{17,113},{2,98},{3,99},{18,114},{19,115},{4... | collective-permute-start | bytes 1105928 | tf_op jit(solution)/shard_map/ppermute | solution.py:56
  19.6 3.1 %collective-permute-start.5 = (bf16[80,1152]{1,0:T(8,128)(2,1)S(1)}, bf16[80,1152]{1,0:T(8,128)(2,1)S(1)}, u32[]{:S(2)}, u32[]{:S(2)}) collective-permute-start(bf16[80,1152]{1,0:T(8,128)(2,1)S(1)} %slice.17), channel_id=1, source_target_pairs={{0,12},{1,13},{16,28},{17,29},{2,14},{3,15},{18,30},{19,31},{4,0},... | collective-permute-start | bytes 552968 | tf_op jit(solution)/shard_map/ppermute | solution.py:56
  23.7 3.1 %collective-permute-start.8 = (bf16[176,1152]{1,0:T(8,128)(2,1)S(1)}, bf16[176,1152]{1,0:T(8,128)(2,1)S(1)}, u32[]{:S(2)}, u32[]{:S(2)}) collective-permute-start(bf16[176,1152]{1,0:T(8,128)(2,1)S(1)} %collective-permute-done.2.refs_2_), channel_id=1, source_target_pairs={{0,12},{1,13},{16,28},{17,29},{2,14},{3,15},{18,30},{19,31},{4,0},... | collective-permute-start | bytes 1216520 | tf_op jit(solution)/shard_map/ppermute | solution.py:56
  27.6 2.3 %collective-permute-done.4.refs_5_ = bf16[96,1152]{1,0:T(8,128)(2,1)S(1)} collective-permute-done((bf16[96,1152]{1,0:T(8,128)(2,1)S(1)}, bf16[96,1152]{1,0:T(8,128)(2,1)S(1)}, u32[]{:S(2)}, u32[]{:S(2)}) %collective-permute-start.4) | collective-permute-done | bytes 221216 | tf_op jit(solution)/shard_map/ppermute | solution.py:56
  30.6 1.7 %collective-permute-start.15 = (bf16[144,1280]{1,0:T(8,128)(2,1)S(1)}, bf16[144,1280]{1,0:T(8,128)(2,1)S(1)}, u32[]{:S(2)}, u32[]{:S(2)}) collective-permute-start(bf16[144,1280]{1,0:T(8,128)(2,1)S(1)} %collective-permute-done.9.refs_2_), channel_id=1, source_target_pairs={{0,32},{1,33},{16,48},{17,49},{2,34},{3,35},{18,50},{19,51},{4,36}... | collective-permute-start | bytes 1105928 | tf_op jit(solution)/shard_map/ppermute | solution.py:56
  33.4 6.0 %collective-permute-done.7.refs_3_ = bf16[176,1152]{1,0:T(8,128)(2,1)S(1)} collective-permute-done((bf16[176,1152]{1,0:T(8,128)(2,1)S(1)}, bf16[176,1152]{1,0:T(8,128)(2,1)S(1)}, u32[]{:S(2)}, u32[]{:S(2)}) %collective-permute-start.7) | collective-permute-done | bytes 405536 | tf_op jit(solution)/shard_map/ppermute | solution.py:56
  39.5 2.1 %collective-permute-start.13 = (bf16[96,1152]{1,0:T(8,128)(2,1)S(1)}, bf16[96,1152]{1,0:T(8,128)(2,1)S(1)}, u32[]{:S(2)}, u32[]{:S(2)}) collective-permute-start(bf16[96,1152]{1,0:T(8,128)(2,1)S(1)} %slice.14), channel_id=1, source_target_pairs={{0,4},{1,5},{16,20},{17,21},{2,6},{3,7},{18,22},{19,23},{4,8},{5,9... | collective-permute-start | bytes 663560 | tf_op jit(solution)/shard_map/ppermute | solution.py:56
  41.8 1.7 %text_units.1 = (bf16[1152,1280]{1,0:T(8,128)(2,1)S(1)}, bf16[1152,1280]{1,0:T(8,128)(2,1)S(1)}, f32[1,1280]{1,0:T(1,128)S(1)}) custom-call(s32[8]{0:T(128)S(1)} %stack.41.place, bf16[144,1280]{1,0:T(8,128)(2,1)S(1)} %bitcast.15, bf16[144,1280]{1,0:T(8,128)(2,1)S(1)} %collective-permute-done.1.refs_0_.refs_1_, ...), custom_call_target="tpu_custom_call" | custom-call | flops 40000000000 | bytes 5898240 | tf_op jit(solution)/shard_map/text_units/pallas_call | solution.py:125
  43.6 1.4 %collective-permute-done.14.refs_6_ = bf16[80,1152]{1,0:T(8,128)(2,1)S(1)} collective-permute-done((bf16[80,1152]{1,0:T(8,128)(2,1)S(1)}, bf16[80,1152]{1,0:T(8,128)(2,1)S(1)}, u32[]{:S(2)}, u32[]{:S(2)}) %collective-permute-start.14) | collective-permute-done | bytes 184352 | tf_op jit(solution)/shard_map/ppermute | solution.py:56
  45.0 1.7 %collective-permute-done.13.refs_5_ = bf16[96,1152]{1,0:T(8,128)(2,1)S(1)} collective-permute-done((bf16[96,1152]{1,0:T(8,128)(2,1)S(1)}, bf16[96,1152]{1,0:T(8,128)(2,1)S(1)}, u32[]{:S(2)}, u32[]{:S(2)}) %collective-permute-start.13) | collective-permute-done | bytes 221216 | tf_op jit(solution)/shard_map/ppermute | solution.py:56
  47.1 5.9 %weights.2 = (bf16[1280,1152]{1,0:T(8,128)(2,1)S(1)}, bf16[1280,1280]{1,0:T(8,128)(2,1)S(1)}, bf16[640,1280]{1,0:T(8,128)(2,1)S(1)}) custom-call(f32[2]{0:T(128)S(1)} %pad_maximum_fusion.2.refs_0_, s32[1]{0:T(128)} %bitcast.refs_1_, bf16[176,1152]{1,0:T(8,128)(2,1)S(1)} %get-tuple-element.66.value.refs_2_, ...), custom_call_target="tpu_custom_call" | custom-call | flops 8000000000 | bytes 6225920 | tf_op jit(solution)/shard_map/weights/pallas_call | solution.py:180
  53.0 5.9 %weights.3 = (bf16[1280,1152]{1,0:T(8,128)(2,1)S(1)}, bf16[1280,1280]{1,0:T(8,128)(2,1)S(1)}, bf16[640,1280]{1,0:T(8,128)(2,1)S(1)}) custom-call(f32[2]{0:T(128)S(1)} %pad_maximum_fusion.2.refs_0_, s32[1]{0:T(128)} %bitcast.refs_1_, bf16[176,1152]{1,0:T(8,128)(2,1)S(1)} %collective-permute-done.2.refs_2_, ...), custom_call_target="tpu_custom_call" | custom-call | flops 8000000000 | bytes 6225920 | tf_op jit(solution)/shard_map/weights/pallas_call | solution.py:180
  60.0 8.8 %text_terms.1 = (f32[144,1280]{1,0:T(8,128)S(1)}, f32[160,1280]{1,0:T(8,128)S(1)}, bf16[144,1280]{1,0:T(8,128)(2,1)S(1)}, bf16[160,1280]{1,0:T(8,128)(2,1)S(1)},...) custom-call(s32[8]{0:T(128)S(1)} %stack.41.place, ...), custom_call_target="tpu_custom_call" | custom-call | flops 7549747200 | bytes 6553600 | tf_op jit(solution)/shard_map/text_terms/pallas_call | solution.py:224
  68.7 1.8 %collective-permute-start.22 = (bf16[144,1280]{1,0:T(8,128)(2,1)S(1)}, bf16[144,1280]{1,0:T(8,128)(2,1)S(1)}, u32[]{:S(2)}, u32[]{:S(2)}) collective-permute-start(bf16[144,1280]{1,0:T(8,128)(2,1)S(1)} %get-tuple-element.102), channel_id=1, source_target_pairs={{0,32},{1,33},{16,48},{17,49},{2,34},{3,35},{18,50},{19,51},{4,36}... | collective-permute-start | bytes 1105928 | tf_op jit(solution)/shard_map/ppermute | solution.py:56
  70.6 1.9 %collective-permute-start.33 = (bf16[160,1280]{1,0:T(8,128)(2,1)S(1)}, bf16[160,1280]{1,0:T(8,128)(2,1)S(1)}, u32[]{:S(2)}, u32[]{:S(2)}) collective-permute-start(bf16[160,1280]{1,0:T(8,128)(2,1)S(1)} %get-tuple-element.125), channel_id=1, source_target_pairs={{0,96},{1,97},{16,112},{17,113},{2,98},{3,99},{18,114},{19,115},{4... | collective-permute-start | bytes 1228808 | tf_op jit(solution)/shard_map/ppermute | solution.py:56
  72.5 8.6 %image_terms.1 = (f32[160,1152]{1,0:T(8,128)S(1)}, f32[160,1152]{1,0:T(8,128)S(1)}, bf16[160,1152]{1,0:T(8,128)(2,1)S(1)}, bf16[160,1152]{1,0:T(8,128)(2,1)S(1)}...) custom-call(bf16[1280,1280]{1,0:T(8,128)(2,1)S(1)} %get-tuple-elemen, ...), custom_call_target="tpu_custom_call" | custom-call | flops 10000000000 | bytes 11796480 | tf_op jit(solution)/shard_map/image_terms/pallas_call | solution.py:254
  81.3 2.0 %collective-permute-start.30 = (bf16[144,1280]{1,0:T(8,128)(2,1)S(1)}, bf16[144,1280]{1,0:T(8,128)(2,1)S(1)}, u32[]{:S(2)}, u32[]{:S(2)}) collective-permute-start(bf16[144,1280]{1,0:T(8,128)(2,1)S(1)} %add_rows.4), channel_id=1, source_target_pairs={{0,32},{1,33},{16,48},{17,49},{2,34},{3,35},{18,50},{19,51},{4,36}... | collective-permute-start | bytes 1105928 | tf_op jit(solution)/shard_map/ppermute | solution.py:56
  84.0 2.5 %collective-permute-start.26 = (bf16[160,1152]{1,0:T(8,128)(2,1)S(1)}, bf16[160,1152]{1,0:T(8,128)(2,1)S(1)}, u32[]{:S(2)}, u32[]{:S(2)}) collective-permute-start(bf16[160,1152]{1,0:T(8,128)(2,1)S(1)} %get-tuple-element.114), channel_id=1, source_target_pairs={{0,12},{1,13},{16,28},{17,29},{2,14},{3,15},{18,30},{19,31},{4,0},... | collective-permute-start | bytes 1105928 | tf_op jit(solution)/shard_map/ppermute | solution.py:56
  86.8 6.1 %collective-permute-done.26.refs_1_ = bf16[160,1152]{1,0:T(8,128)(2,1)S(1)} collective-permute-done((bf16[160,1152]{1,0:T(8,128)(2,1)S(1)}, bf16[160,1152]{1,0:T(8,128)(2,1)S(1)}, u32[]{:S(2)}, u32[]{:S(2)}) %collective-permute-start.26) | collective-permute-done | bytes 368672 | tf_op jit(solution)/shard_map/ppermute | solution.py:56
  93.3 3.5 %collective-permute-start.28 = (bf16[160,1152]{1,0:T(8,128)(2,1)S(1)}, bf16[160,1152]{1,0:T(8,128)(2,1)S(1)}, u32[]{:S(2)}, u32[]{:S(2)}) collective-permute-start(bf16[160,1152]{1,0:T(8,128)(2,1)S(1)} %add_rows.6), channel_id=1, source_target_pairs={{0,12},{1,13},{16,28},{17,29},{2,14},{3,15},{18,30},{19,31},{4,0},... | collective-permute-start | bytes 1105928 | tf_op jit(solution)/shard_map/ppermute | solution.py:56
  97.5 1.1 collective-permute-start.35
  98.8 4.1 %collective-permute-done.27.ahead = bf16[160,1152]{1,0:T(8,128)(2,1)S(1)} collective-permute-done((bf16[160,1152]{1,0:T(8,128)(2,1)S(1)}, bf16[160,1152]{1,0:T(8,128)(2,1)S(1)}, u32[]{:S(2)}, u32[]{:S(2)}) %collective-permute-start.27) | collective-permute-done | bytes 368672 | tf_op jit(solution)/shard_map/ppermute | solution.py:56
  103.0 2.7 %collective-permute-start.29 = (bf16[160,1152]{1,0:T(8,128)(2,1)S(1)}, bf16[160,1152]{1,0:T(8,128)(2,1)S(1)}, u32[]{:S(2)}, u32[]{:S(2)}) collective-permute-start(bf16[160,1152]{1,0:T(8,128)(2,1)S(1)} %add_three.2), channel_id=1, source_target_pairs={{0,2},{1,3},{16,18},{17,19},{2,0},{3,1},{18,16},{19,17},{4,6},{5,7... | collective-permute-start | bytes 1105928 | tf_op jit(solution)/shard_map/ppermute | solution.py:56
  105.7 1.1 collective-permute-start.24
  106.8 2.1 %collective-permute-start.25 = (bf16[160,1152]{1,0:T(8,128)(2,1)S(1)}, bf16[160,1152]{1,0:T(8,128)(2,1)S(1)}, u32[]{:S(2)}, u32[]{:S(2)}) collective-permute-start(bf16[160,1152]{1,0:T(8,128)(2,1)S(1)} %get-tuple-element.111), channel_id=1, source_target_pairs={{0,12},{1,13},{16,28},{17,29},{2,14},{3,15},{18,30},{19,31},{4,0},... | collective-permute-start | bytes 1105928 | tf_op jit(solution)/shard_map/ppermute | solution.py:56
  108.9 1.1 text_final.1
  110.0 5.2 %collective-permute-done.29.given = bf16[160,1152]{1,0:T(8,128)(2,1)S(1)} collective-permute-done((bf16[160,1152]{1,0:T(8,128)(2,1)S(1)}, bf16[160,1152]{1,0:T(8,128)(2,1)S(1)}, u32[]{:S(2)}, u32[]{:S(2)}) %collective-permute-start.29) | collective-permute-done | bytes 368672 | tf_op jit(solution)/shard_map/ppermute | solution.py:56
  115.2 1.1 image_final.1
  (76 shorter events, 12.5 us)
Async XLA Ops:
  0.6 10.8 %collective-permute-start.1 = (bf16[144,1280]{1,0:T(8,128)(2,1)}, bf16[144,1280]{1,0:T(8,128)(2,1)S(1)}, u32[]{:S(2)}, u32[]{:S(2)}) collective-permute-start(bf16[144,1280]{1,0:T(8,128)(2,1)} %bitcast.12), channel_id=1, source_target_pairs={{0,16},{1,17},{16,0},{17,1},{2,18},{3,19},{18,2},{19,3},{4,20},{5,... | collective-permute-start | bytes 1105928 | tf_op jit(solution)/shard_map/ppermute | solution.py:56
  2.6 14.9 %collective-permute-start.11 = (bf16[144,1280]{1,0:T(8,128)(2,1)}, bf16[144,1280]{1,0:T(8,128)(2,1)S(1)}, u32[]{:S(2)}, u32[]{:S(2)}) collective-permute-start(bf16[144,1280]{1,0:T(8,128)(2,1)} %bitcast.13), channel_id=1, source_target_pairs={{0,96},{1,97},{16,112},{17,113},{2,98},{3,99},{18,114},{19,115},{4... | collective-permute-start | bytes 1105928 | tf_op jit(solution)/shard_map/ppermute | solution.py:56
  3.5 14.1 %collective-permute-start.9 = (bf16[144,1280]{1,0:T(8,128)(2,1)}, bf16[144,1280]{1,0:T(8,128)(2,1)S(1)}, u32[]{:S(2)}, u32[]{:S(2)}) collective-permute-start(bf16[144,1280]{1,0:T(8,128)(2,1)} %bitcast.14), channel_id=1, source_target_pairs={{0,32},{1,33},{16,48},{17,49},{2,34},{3,35},{18,50},{19,51},{4,36}... | collective-permute-start | bytes 1105928 | tf_op jit(solution)/shard_map/ppermute | solution.py:56
  7.7 11.9 %collective-permute-start.3 = (bf16[176,1152]{1,0:T(8,128)(2,1)S(1)}, bf16[176,1152]{1,0:T(8,128)(2,1)S(1)}, u32[]{:S(2)}, u32[]{:S(2)}) collective-permute-start(bf16[176,1152]{1,0:T(8,128)(2,1)S(1)} %get-tuple-element.66.value.refs_2_), channel_id=1, source_target_pairs={{0,12},{1,13},{16,28},{17,29},{2,14},{3,15},{18,30},{19,31},{4,0},... | collective-permute-start | bytes 1216520 | tf_op jit(solution)/shard_map/ppermute | solution.py:56
  10.8 11.9 %collective-permute-start = (bf16[176,1152]{1,0:T(8,128)(2,1)S(1)}, bf16[176,1152]{1,0:T(8,128)(2,1)S(1)}, u32[]{:S(2)}, u32[]{:S(2)}) collective-permute-start(bf16[176,1152]{1,0:T(8,128)(2,1)S(1)} %get-tuple-element.66.value.refs_2_), channel_id=1, source_target_pairs={{0,4},{1,5},{16,20},{17,21},{2,6},{3,7},{18,22},{19,23},{4,8},{5,9... | collective-permute-start | bytes 1216520 | tf_op jit(solution)/shard_map/ppermute | solution.py:56
  11.5 12.3 %collective-permute-start.2 = (bf16[176,1152]{1,0:T(8,128)(2,1)S(1)}, bf16[176,1152]{1,0:T(8,128)(2,1)S(1)}, u32[]{:S(2)}, u32[]{:S(2)}) collective-permute-start(bf16[176,1152]{1,0:T(8,128)(2,1)S(1)} %hold.1), channel_id=1, source_target_pairs={{0,2},{1,3},{16,18},{17,19},{2,0},{3,1},{18,16},{19,17},{4,6},{5,7... | collective-permute-start | bytes 1216520 | tf_op jit(solution)/shard_map/ppermute | solution.py:56
  17.5 15.8 %collective-permute-start.10 = (bf16[144,1280]{1,0:T(8,128)(2,1)S(1)}, bf16[144,1280]{1,0:T(8,128)(2,1)S(1)}, u32[]{:S(2)}, u32[]{:S(2)}) collective-permute-start(bf16[144,1280]{1,0:T(8,128)(2,1)S(1)} %collective-permute-done.1.refs_0_.refs_1_), channel_id=1, source_target_pairs={{0,32},{1,33},{16,48},{17,49},{2,34},{3,35},{18,50},{19,51},{4,36}... | collective-permute-start | bytes 1105928 | tf_op jit(solution)/shard_map/ppermute | solution.py:56
  18.0 14.3 %collective-permute-start.12 = (bf16[144,1280]{1,0:T(8,128)(2,1)S(1)}, bf16[144,1280]{1,0:T(8,128)(2,1)S(1)}, u32[]{:S(2)}, u32[]{:S(2)}) collective-permute-start(bf16[144,1280]{1,0:T(8,128)(2,1)S(1)} %collective-permute-done.1.refs_0_.refs_1_), channel_id=1, source_target_pairs={{0,96},{1,97},{16,112},{17,113},{2,98},{3,99},{18,114},{19,115},{4... | collective-permute-start | bytes 1105928 | tf_op jit(solution)/shard_map/ppermute | solution.py:56
  19.6 11.0 %collective-permute-start.5 = (bf16[80,1152]{1,0:T(8,128)(2,1)S(1)}, bf16[80,1152]{1,0:T(8,128)(2,1)S(1)}, u32[]{:S(2)}, u32[]{:S(2)}) collective-permute-start(bf16[80,1152]{1,0:T(8,128)(2,1)S(1)} %slice.17), channel_id=1, source_target_pairs={{0,12},{1,13},{16,28},{17,29},{2,14},{3,15},{18,30},{19,31},{4,0},... | collective-permute-start | bytes 552968 | tf_op jit(solution)/shard_map/ppermute | solution.py:56
  23.7 15.7 %collective-permute-start.8 = (bf16[176,1152]{1,0:T(8,128)(2,1)S(1)}, bf16[176,1152]{1,0:T(8,128)(2,1)S(1)}, u32[]{:S(2)}, u32[]{:S(2)}) collective-permute-start(bf16[176,1152]{1,0:T(8,128)(2,1)S(1)} %collective-permute-done.2.refs_2_), channel_id=1, source_target_pairs={{0,12},{1,13},{16,28},{17,29},{2,14},{3,15},{18,30},{19,31},{4,0},... | collective-permute-start | bytes 1216520 | tf_op jit(solution)/shard_map/ppermute | solution.py:56
  29.9 9.5 %collective-permute-start.7 = (bf16[176,1152]{1,0:T(8,128)(2,1)S(1)}, bf16[176,1152]{1,0:T(8,128)(2,1)S(1)}, u32[]{:S(2)}, u32[]{:S(2)}) collective-permute-start(bf16[176,1152]{1,0:T(8,128)(2,1)S(1)} %collective-permute-done.2.refs_2_), channel_id=1, source_target_pairs={{0,4},{1,5},{16,20},{17,21},{2,6},{3,7},{18,22},{19,23},{4,8},{5,9... | collective-permute-start | bytes 1216520 | tf_op jit(solution)/shard_map/ppermute | solution.py:56
  30.6 11.1 %collective-permute-start.15 = (bf16[144,1280]{1,0:T(8,128)(2,1)S(1)}, bf16[144,1280]{1,0:T(8,128)(2,1)S(1)}, u32[]{:S(2)}, u32[]{:S(2)}) collective-permute-start(bf16[144,1280]{1,0:T(8,128)(2,1)S(1)} %collective-permute-done.9.refs_2_), channel_id=1, source_target_pairs={{0,32},{1,33},{16,48},{17,49},{2,34},{3,35},{18,50},{19,51},{4,36}... | collective-permute-start | bytes 1105928 | tf_op jit(solution)/shard_map/ppermute | solution.py:56
  32.3 9.5 %collective-permute-start.16 = (bf16[144,1280]{1,0:T(8,128)(2,1)S(1)}, bf16[144,1280]{1,0:T(8,128)(2,1)S(1)}, u32[]{:S(2)}, u32[]{:S(2)}) collective-permute-start(bf16[144,1280]{1,0:T(8,128)(2,1)S(1)} %collective-permute-done.12.refs_5_), channel_id=1, source_target_pairs={{0,96},{1,97},{16,112},{17,113},{2,98},{3,99},{18,114},{19,115},{4... | collective-permute-start | bytes 1105928 | tf_op jit(solution)/shard_map/ppermute | solution.py:56
  33.4 13.7 %collective-permute-start.6 = (bf16[704,1152]{1,0:T(8,128)(2,1)}, bf16[704,1152]{1,0:T(8,128)(2,1)S(1)}, u32[]{:S(2)}, u32[]{:S(2)}) collective-permute-start(bf16[704,1152]{1,0:T(8,128)(2,1)} %constant_dynamic-update-slice_fusion), channel_id=1, source_target_pairs={{0,1},{1,0},{16,17},{17,16},{2,3},{3,2},{18,19},{19,18},{4,5},{5,4... | collective-permute-start | bytes 4866056 | tf_op jit(solution)/shard_map/ppermute | solution.py:56
  41.7 11.3 %collective-permute-start.18 = (bf16[528,1152]{1,0:T(8,128)(2,1)S(1)}, bf16[528,1152]{1,0:T(8,128)(2,1)S(1)}, u32[]{:S(2)}, u32[]{:S(2)}) collective-permute-start(bf16[528,1152]{1,0:T(8,128)(2,1)S(1)} %pad_maximum_fusion), channel_id=1, source_target_pairs={{0,1},{1,0},{16,17},{17,16},{2,3},{3,2},{18,19},{19,18},{4,5},{5,4... | collective-permute-start | bytes 3649544 | tf_op jit(solution)/shard_map/ppermute | solution.py:56
  58.9 13.7 %collective-permute-start.21 = (bf16[1152,1280]{1,0:T(8,128)(2,1)S(1)}, bf16[1152,1280]{1,0:T(8,128)(2,1)S(1)}, u32[]{:S(2)}, u32[]{:S(2)}) collective-permute-start(bf16[1152,1280]{1,0:T(8,128)(2,1)S(1)} %get-tuple-element.96.refs_8_.refs_9_.refs_4_), channel_id=1, source_target_pairs={{0,1},{1,0},{16,17},{17,16},{2,3},{3,2},{18,19},{19,18},{4,5},{5,4... | collective-permute-start | bytes 8847368 | tf_op jit(solution)/shard_map/ppermute | solution.py:56
  59.5 9.3 %collective-permute-start.20 = (bf16[640,1280]{1,0:T(8,128)(2,1)S(1)}, bf16[640,1280]{1,0:T(8,128)(2,1)S(1)}, u32[]{:S(2)}, u32[]{:S(2)}) collective-permute-start(bf16[640,1280]{1,0:T(8,128)(2,1)S(1)} %get-tuple-element.83), channel_id=1, source_target_pairs={{0,1},{1,0},{16,17},{17,16},{2,3},{3,2},{18,19},{19,18},{4,5},{5,4... | collective-permute-start | bytes 4915208 | tf_op jit(solution)/shard_map/ppermute | solution.py:56
  59.6 13.0 %collective-permute-start.17 = (bf16[640,1280]{1,0:T(8,128)(2,1)S(1)}, bf16[640,1280]{1,0:T(8,128)(2,1)S(1)}, u32[]{:S(2)}, u32[]{:S(2)}) collective-permute-start(bf16[640,1280]{1,0:T(8,128)(2,1)S(1)} %get-tuple-element.80), channel_id=1, source_target_pairs={{0,1},{1,0},{16,17},{17,16},{2,3},{3,2},{18,19},{19,18},{4,5},{5,4... | collective-permute-start | bytes 4915208 | tf_op jit(solution)/shard_map/ppermute | solution.py:56
  68.7 12.5 %collective-permute-start.22 = (bf16[144,1280]{1,0:T(8,128)(2,1)S(1)}, bf16[144,1280]{1,0:T(8,128)(2,1)S(1)}, u32[]{:S(2)}, u32[]{:S(2)}) collective-permute-start(bf16[144,1280]{1,0:T(8,128)(2,1)S(1)} %get-tuple-element.102), channel_id=1, source_target_pairs={{0,32},{1,33},{16,48},{17,49},{2,34},{3,35},{18,50},{19,51},{4,36}... | collective-permute-start | bytes 1105928 | tf_op jit(solution)/shard_map/ppermute | solution.py:56
  70.5 22.8 %collective-permute-start.32 = (bf16[160,1280]{1,0:T(8,128)(2,1)S(1)}, bf16[160,1280]{1,0:T(8,128)(2,1)S(1)}, u32[]{:S(2)}, u32[]{:S(2)}) collective-permute-start(bf16[160,1280]{1,0:T(8,128)(2,1)S(1)} %get-tuple-element.123), channel_id=1, source_target_pairs={{0,32},{1,33},{16,48},{17,49},{2,34},{3,35},{18,50},{19,51},{4,36}... | collective-permute-start | bytes 1228808 | tf_op jit(solution)/shard_map/ppermute | solution.py:56
  70.6 16.0 %collective-permute-start.33 = (bf16[160,1280]{1,0:T(8,128)(2,1)S(1)}, bf16[160,1280]{1,0:T(8,128)(2,1)S(1)}, u32[]{:S(2)}, u32[]{:S(2)}) collective-permute-start(bf16[160,1280]{1,0:T(8,128)(2,1)S(1)} %get-tuple-element.125), channel_id=1, source_target_pairs={{0,96},{1,97},{16,112},{17,113},{2,98},{3,99},{18,114},{19,115},{4... | collective-permute-start | bytes 1228808 | tf_op jit(solution)/shard_map/ppermute | solution.py:56
  81.3 25.5 %collective-permute-start.30 = (bf16[144,1280]{1,0:T(8,128)(2,1)S(1)}, bf16[144,1280]{1,0:T(8,128)(2,1)S(1)}, u32[]{:S(2)}, u32[]{:S(2)}) collective-permute-start(bf16[144,1280]{1,0:T(8,128)(2,1)S(1)} %add_rows.4), channel_id=1, source_target_pairs={{0,32},{1,33},{16,48},{17,49},{2,34},{3,35},{18,50},{19,51},{4,36}... | collective-permute-start | bytes 1105928 | tf_op jit(solution)/shard_map/ppermute | solution.py:56
  83.3 15.3 %collective-permute-start.23 = (bf16[160,1152]{1,0:T(8,128)(2,1)S(1)}, bf16[160,1152]{1,0:T(8,128)(2,1)S(1)}, u32[]{:S(2)}, u32[]{:S(2)}) collective-permute-start(bf16[160,1152]{1,0:T(8,128)(2,1)S(1)} %get-tuple-element.108), channel_id=1, source_target_pairs={{0,4},{1,5},{16,20},{17,21},{2,6},{3,7},{18,22},{19,23},{4,8},{5,9... | collective-permute-start | bytes 1105928 | tf_op jit(solution)/shard_map/ppermute | solution.py:56
  84.0 8.9 %collective-permute-start.26 = (bf16[160,1152]{1,0:T(8,128)(2,1)S(1)}, bf16[160,1152]{1,0:T(8,128)(2,1)S(1)}, u32[]{:S(2)}, u32[]{:S(2)}) collective-permute-start(bf16[160,1152]{1,0:T(8,128)(2,1)S(1)} %get-tuple-element.114), channel_id=1, source_target_pairs={{0,12},{1,13},{16,28},{17,29},{2,14},{3,15},{18,30},{19,31},{4,0},... | collective-permute-start | bytes 1105928 | tf_op jit(solution)/shard_map/ppermute | solution.py:56
  86.7 10.7 %collective-permute-start.34 = (bf16[160,1280]{1,0:T(8,128)(2,1)S(1)}, bf16[160,1280]{1,0:T(8,128)(2,1)S(1)}, u32[]{:S(2)}, u32[]{:S(2)}) collective-permute-start(bf16[160,1280]{1,0:T(8,128)(2,1)S(1)} %add_rows.7), channel_id=1, source_target_pairs={{0,96},{1,97},{16,112},{17,113},{2,98},{3,99},{18,114},{19,115},{4... | collective-permute-start | bytes 1228808 | tf_op jit(solution)/shard_map/ppermute | solution.py:56
  93.0 9.9 %collective-permute-start.27 = (bf16[160,1152]{1,0:T(8,128)(2,1)S(1)}, bf16[160,1152]{1,0:T(8,128)(2,1)S(1)}, u32[]{:S(2)}, u32[]{:S(2)}) collective-permute-start(bf16[160,1152]{1,0:T(8,128)(2,1)S(1)} %get-tuple-element.117), channel_id=1, source_target_pairs={{0,4},{1,5},{16,20},{17,21},{2,6},{3,7},{18,22},{19,23},{4,8},{5,9... | collective-permute-start | bytes 1105928 | tf_op jit(solution)/shard_map/ppermute | solution.py:56
  93.3 9.6 %collective-permute-start.28 = (bf16[160,1152]{1,0:T(8,128)(2,1)S(1)}, bf16[160,1152]{1,0:T(8,128)(2,1)S(1)}, u32[]{:S(2)}, u32[]{:S(2)}) collective-permute-start(bf16[160,1152]{1,0:T(8,128)(2,1)S(1)} %add_rows.6), channel_id=1, source_target_pairs={{0,12},{1,13},{16,28},{17,29},{2,14},{3,15},{18,30},{19,31},{4,0},... | collective-permute-start | bytes 1105928 | tf_op jit(solution)/shard_map/ppermute | solution.py:56
  97.5 11.5 %collective-permute-start.35 = (bf16[160,1280]{1,0:T(8,128)(2,1)S(1)}, bf16[160,1280]{1,0:T(8,128)(2,1)S(1)}, u32[]{:S(2)}, u32[]{:S(2)}) collective-permute-start(bf16[160,1280]{1,0:T(8,128)(2,1)S(1)} %add_three.3.gave), channel_id=1, source_target_pairs={{0,16},{1,17},{16,0},{17,1},{2,18},{3,19},{18,2},{19,3},{4,20},{5,... | collective-permute-start | bytes 1228808 | tf_op jit(solution)/shard_map/ppermute | solution.py:56
  98.7 10.3 %collective-permute-start.31 = (bf16[144,1280]{1,0:T(8,128)(2,1)S(1)}, bf16[144,1280]{1,0:T(8,128)(2,1)S(1)}, u32[]{:S(2)}, u32[]{:S(2)}) collective-permute-start(bf16[144,1280]{1,0:T(8,128)(2,1)S(1)} %get-tuple-element.121), channel_id=1, source_target_pairs={{0,96},{1,97},{16,112},{17,113},{2,98},{3,99},{18,114},{19,115},{4... | collective-permute-start | bytes 1105928 | tf_op jit(solution)/shard_map/ppermute | solution.py:56
  103.0 12.2 %collective-permute-start.29 = (bf16[160,1152]{1,0:T(8,128)(2,1)S(1)}, bf16[160,1152]{1,0:T(8,128)(2,1)S(1)}, u32[]{:S(2)}, u32[]{:S(2)}) collective-permute-start(bf16[160,1152]{1,0:T(8,128)(2,1)S(1)} %add_three.2), channel_id=1, source_target_pairs={{0,2},{1,3},{16,18},{17,19},{2,0},{3,1},{18,16},{19,17},{4,6},{5,7... | collective-permute-start | bytes 1105928 | tf_op jit(solution)/shard_map/ppermute | solution.py:56
  105.7 9.5 %collective-permute-start.24 = (bf16[160,1152]{1,0:T(8,128)(2,1)S(1)}, bf16[160,1152]{1,0:T(8,128)(2,1)S(1)}, u32[]{:S(2)}, u32[]{:S(2)}) collective-permute-start(bf16[160,1152]{1,0:T(8,128)(2,1)S(1)} %add_rows.5), channel_id=1, source_target_pairs={{0,4},{1,5},{16,20},{17,21},{2,6},{3,7},{18,22},{19,23},{4,8},{5,9... | collective-permute-start | bytes 1105928 | tf_op jit(solution)/shard_map/ppermute | solution.py:56
  106.8 8.4 %collective-permute-start.25 = (bf16[160,1152]{1,0:T(8,128)(2,1)S(1)}, bf16[160,1152]{1,0:T(8,128)(2,1)S(1)}, u32[]{:S(2)}, u32[]{:S(2)}) collective-permute-start(bf16[160,1152]{1,0:T(8,128)(2,1)S(1)} %get-tuple-element.111), channel_id=1, source_target_pairs={{0,12},{1,13},{16,28},{17,29},{2,14},{3,15},{18,30},{19,31},{4,0},... | collective-permute-start | bytes 1105928 | tf_op jit(solution)/shard_map/ppermute | solution.py:56
  (8 other events, 48.6 us)
where the time goes:
time: 117 us; the launch traced here: 116 us
  starting transfers between devices  46.1 us (39%)
  Pallas kernels  33.9 us (29%)
  waiting for transfers between devices  28.3 us (24%)
  local copies, waits for them, and re-layouts  5.58 us (5%)
  between operations  2.23 us (2%)
    ppermute x36, starting transfers between devices, send(): return lax.ppermute(value, AXES, MOVES[move])  46.1 us
    ppermute x36, waiting for transfers between devices, send(): return lax.ppermute(value, AXES, MOVES[move])  28.3 us
    pallas_call x2, Pallas kernels, weights(): pl.pallas_call(lambda *refs: weight_kernel(rows, *refs), out_shape=[jax.S...  11.8 us
    pallas_call x1, Pallas kernels, text_terms(): pl.pallas_call(text_back_kernel, out_shape=[jax.ShapeDtypeStruct((width /...  8.75 us
    pallas_call x1, Pallas kernels, image_terms(): pl.pallas_call(lambda *refs: image_back_kernel(rows, *refs), out_shape=[j...  8.64 us
    unnamed x12, local copies, waits for them, and re-layouts  4.73 us
  transfers between devices with their start and end apart: 36, of which 10 were waited for; matrix products, arithmetic and copies ran while one was open for 4% of the time, Pallas kernels for 23%

commit v1 on v0

--- a/solution.py
+++ b/solution.py
@@ -415,7 +415,8 @@
     x_ahead1 = send(x_ahead[1], ("x", 1))
     y_relay1, y_relay0 = send(y_far[1], ("y", -1)), send(y_far[0], ("y", 1))
     x_back0, x_back1, x_ahead0, _ = lax.optimization_barrier((*x_back, x_ahead[0], y_own[0]))
-    x_back1, x_ahead0 = add_rows(x_back1, x_relay1, 0), add_rows(x_ahead0, x_relay0, 0)
+    x_back1, x_ahead0 = lax.optimization_barrier((add_rows(x_back1, x_relay1, 0), x_ahead0))
+    x_ahead0 = add_rows(x_ahead0, x_relay0, 0)
     x_ahead0, y_back0, y_back1, y_ahead0, y_ahead1 = lax.optimization_barrier(
         (x_ahead0, *y_back, *y_ahead)
     )

time: 117 us -> 117 us (level)
  transfers between devices with their start and end apart: 36 -> 36, of which waited for: 10 -> 11; matrix products, arithmetic and copies ran while one was open for 4% -> 4% of each run, Pallas kernels for 23% -> 23%
where the time goes in v1:
time: 117 us; the launch traced here: 115 us
  starting transfers between devices  46 us (39%)
  Pallas kernels  34 us (29%)
  waiting for transfers between devices  27.4 us (23%)
  local copies, waits for them, and re-layouts  5.58 us (5%)
  between operations  2.23 us (2%)
    ppermute x36, starting transfers between devices, send(): return lax.ppermute(value, AXES, MOVES[move])  46 us
    ppermute x36, waiting for transfers between devices, send(): return lax.ppermute(value, AXES, MOVES[move])  27.4 us
    pallas_call x2, Pallas kernels, weights(): pl.pallas_call(lambda *refs: weight_kernel(rows, *refs), out_shape=[jax.S...  11.8 us
    pallas_call x1, Pallas kernels, text_terms(): pl.pallas_call(text_back_kernel, out_shape=[jax.ShapeDtypeStruct((width /...  8.75 us
    pallas_call x1, Pallas kernels, image_terms(): pl.pallas_call(lambda *refs: image_back_kernel(rows, *refs), out_shape=[j...  8.64 us
    unnamed x12, local copies, waits for them, and re-layouts  4.73 us
  transfers between devices with their start and end apart: 36, of which 11 were waited for; matrix products, arithmetic and copies ran while one was open for 4% of the time, Pallas kernels for 23%

profile of v1, /device:TPU:6, one launch (start us, length us, event | category | flops | bytes accessed | tf_op | source)
XLA Modules:
  0.0 115.4 jit_solution(15694336425906936209)
XLA Ops:
  0.6 2.0 %collective-permute-start.1 = (bf16[144,1280]{1,0:T(8,128)(2,1)}, bf16[144,1280]{1,0:T(8,128)(2,1)S(1)}, u32[]{:S(2)}, u32[]{:S(2)}) collective-permute-start(bf16[144,1280]{1,0:T(8,128)(2,1)} %bitcast.12), channel_id=1, source_target_pairs={{0,16},{1,17},{16,0},{17,1},{2,18},{3,19},{18,2},{19,3},{4,20},{5,... | collective-permute-start | bytes 1105928 | tf_op jit(solution)/shard_map/ppermute | solution.py:56
  3.5 2.4 %collective-permute-start.9 = (bf16[144,1280]{1,0:T(8,128)(2,1)}, bf16[144,1280]{1,0:T(8,128)(2,1)S(1)}, u32[]{:S(2)}, u32[]{:S(2)}) collective-permute-start(bf16[144,1280]{1,0:T(8,128)(2,1)} %bitcast.14), channel_id=1, source_target_pairs={{0,32},{1,33},{16,48},{17,49},{2,34},{3,35},{18,50},{19,51},{4,36}... | collective-permute-start | bytes 1105928 | tf_op jit(solution)/shard_map/ppermute | solution.py:56
  5.9 1.0 copy-done
  7.7 3.1 %collective-permute-start.3 = (bf16[176,1152]{1,0:T(8,128)(2,1)S(1)}, bf16[176,1152]{1,0:T(8,128)(2,1)S(1)}, u32[]{:S(2)}, u32[]{:S(2)}) collective-permute-start(bf16[176,1152]{1,0:T(8,128)(2,1)S(1)} %get-tuple-element.68.value.refs_2_), channel_id=1, source_target_pairs={{0,12},{1,13},{16,28},{17,29},{2,14},{3,15},{18,30},{19,31},{4,0},... | collective-permute-start | bytes 1216520 | tf_op jit(solution)/shard_map/ppermute | solution.py:56
  11.5 3.8 %collective-permute-start.2 = (bf16[176,1152]{1,0:T(8,128)(2,1)S(1)}, bf16[176,1152]{1,0:T(8,128)(2,1)S(1)}, u32[]{:S(2)}, u32[]{:S(2)}) collective-permute-start(bf16[176,1152]{1,0:T(8,128)(2,1)S(1)} %hold.1), channel_id=1, source_target_pairs={{0,2},{1,3},{16,18},{17,19},{2,0},{3,1},{18,16},{19,17},{4,6},{5,7... | collective-permute-start | bytes 1216520 | tf_op jit(solution)/shard_map/ppermute | solution.py:56
  18.0 1.5 %collective-permute-start.12 = (bf16[144,1280]{1,0:T(8,128)(2,1)S(1)}, bf16[144,1280]{1,0:T(8,128)(2,1)S(1)}, u32[]{:S(2)}, u32[]{:S(2)}) collective-permute-start(bf16[144,1280]{1,0:T(8,128)(2,1)S(1)} %collective-permute-done.1.refs_0_.refs_1_), channel_id=1, source_target_pairs={{0,96},{1,97},{16,112},{17,113},{2,98},{3,99},{18,114},{19,115},{4... | collective-permute-start | bytes 1105928 | tf_op jit(solution)/shard_map/ppermute | solution.py:56
  19.6 3.1 %collective-permute-start.5 = (bf16[80,1152]{1,0:T(8,128)(2,1)S(1)}, bf16[80,1152]{1,0:T(8,128)(2,1)S(1)}, u32[]{:S(2)}, u32[]{:S(2)}) collective-permute-start(bf16[80,1152]{1,0:T(8,128)(2,1)S(1)} %slice.17), channel_id=1, source_target_pairs={{0,12},{1,13},{16,28},{17,29},{2,14},{3,15},{18,30},{19,31},{4,0},... | collective-permute-start | bytes 552968 | tf_op jit(solution)/shard_map/ppermute | solution.py:56
  23.7 3.1 %collective-permute-start.8 = (bf16[176,1152]{1,0:T(8,128)(2,1)S(1)}, bf16[176,1152]{1,0:T(8,128)(2,1)S(1)}, u32[]{:S(2)}, u32[]{:S(2)}) collective-permute-start(bf16[176,1152]{1,0:T(8,128)(2,1)S(1)} %collective-permute-done.2.refs_2_), channel_id=1, source_target_pairs={{0,12},{1,13},{16,28},{17,29},{2,14},{3,15},{18,30},{19,31},{4,0},... | collective-permute-start | bytes 1216520 | tf_op jit(solution)/shard_map/ppermute | solution.py:56
  27.6 2.3 %collective-permute-done.4.refs_5_ = bf16[96,1152]{1,0:T(8,128)(2,1)S(1)} collective-permute-done((bf16[96,1152]{1,0:T(8,128)(2,1)S(1)}, bf16[96,1152]{1,0:T(8,128)(2,1)S(1)}, u32[]{:S(2)}, u32[]{:S(2)}) %collective-permute-start.4) | collective-permute-done | bytes 221216 | tf_op jit(solution)/shard_map/ppermute | solution.py:56
  30.6 1.7 %collective-permute-start.15 = (bf16[144,1280]{1,0:T(8,128)(2,1)S(1)}, bf16[144,1280]{1,0:T(8,128)(2,1)S(1)}, u32[]{:S(2)}, u32[]{:S(2)}) collective-permute-start(bf16[144,1280]{1,0:T(8,128)(2,1)S(1)} %collective-permute-done.9.refs_2_), channel_id=1, source_target_pairs={{0,32},{1,33},{16,48},{17,49},{2,34},{3,35},{18,50},{19,51},{4,36}... | collective-permute-start | bytes 1105928 | tf_op jit(solution)/shard_map/ppermute | solution.py:56
  33.4 6.0 %collective-permute-done.7.refs_3_ = bf16[176,1152]{1,0:T(8,128)(2,1)S(1)} collective-permute-done((bf16[176,1152]{1,0:T(8,128)(2,1)S(1)}, bf16[176,1152]{1,0:T(8,128)(2,1)S(1)}, u32[]{:S(2)}, u32[]{:S(2)}) %collective-permute-start.7) | collective-permute-done | bytes 405536 | tf_op jit(solution)/shard_map/ppermute | solution.py:56
  39.5 2.1 %collective-permute-start.13 = (bf16[96,1152]{1,0:T(8,128)(2,1)S(1)}, bf16[96,1152]{1,0:T(8,128)(2,1)S(1)}, u32[]{:S(2)}, u32[]{:S(2)}) collective-permute-start(bf16[96,1152]{1,0:T(8,128)(2,1)S(1)} %slice.14), channel_id=1, source_target_pairs={{0,4},{1,5},{16,20},{17,21},{2,6},{3,7},{18,22},{19,23},{4,8},{5,9... | collective-permute-start | bytes 663560 | tf_op jit(solution)/shard_map/ppermute | solution.py:56
  41.8 1.7 %text_units.1 = (bf16[1152,1280]{1,0:T(8,128)(2,1)S(1)}, bf16[1152,1280]{1,0:T(8,128)(2,1)S(1)}, f32[1,1280]{1,0:T(1,128)S(1)}) custom-call(s32[8]{0:T(128)S(1)} %stack.41.place, bf16[144,1280]{1,0:T(8,128)(2,1)S(1)} %bitcast.15, bf16[144,1280]{1,0:T(8,128)(2,1)S(1)} %collective-permute-done.1.refs_0_.refs_1_, ...), custom_call_target="tpu_custom_call" | custom-call | flops 40000000000 | bytes 5898240 | tf_op jit(solution)/shard_map/text_units/pallas_call | solution.py:125
  43.6 1.5 %collective-permute-done.14.refs_6_ = bf16[80,1152]{1,0:T(8,128)(2,1)S(1)} collective-permute-done((bf16[80,1152]{1,0:T(8,128)(2,1)S(1)}, bf16[80,1152]{1,0:T(8,128)(2,1)S(1)}, u32[]{:S(2)}, u32[]{:S(2)}) %collective-permute-start.14) | collective-permute-done | bytes 184352 | tf_op jit(solution)/shard_map/ppermute | solution.py:56
  45.0 1.7 %collective-permute-done.13.refs_5_ = bf16[96,1152]{1,0:T(8,128)(2,1)S(1)} collective-permute-done((bf16[96,1152]{1,0:T(8,128)(2,1)S(1)}, bf16[96,1152]{1,0:T(8,128)(2,1)S(1)}, u32[]{:S(2)}, u32[]{:S(2)}) %collective-permute-start.13) | collective-permute-done | bytes 221216 | tf_op jit(solution)/shard_map/ppermute | solution.py:56
  47.1 5.9 %weights.2 = (bf16[1280,1152]{1,0:T(8,128)(2,1)S(1)}, bf16[1280,1280]{1,0:T(8,128)(2,1)S(1)}, bf16[640,1280]{1,0:T(8,128)(2,1)S(1)}) custom-call(f32[2]{0:T(128)S(1)} %pad_maximum_fusion.2.refs_0_, s32[1]{0:T(128)} %bitcast.refs_1_, bf16[176,1152]{1,0:T(8,128)(2,1)S(1)} %get-tuple-element.68.value.refs_2_, ...), custom_call_target="tpu_custom_call" | custom-call | flops 8000000000 | bytes 6225920 | tf_op jit(solution)/shard_map/weights/pallas_call | solution.py:180
  53.0 5.9 %weights.3 = (bf16[1280,1152]{1,0:T(8,128)(2,1)S(1)}, bf16[1280,1280]{1,0:T(8,128)(2,1)S(1)}, bf16[640,1280]{1,0:T(8,128)(2,1)S(1)}) custom-call(f32[2]{0:T(128)S(1)} %pad_maximum_fusion.2.refs_0_, s32[1]{0:T(128)} %bitcast.refs_1_, bf16[176,1152]{1,0:T(8,128)(2,1)S(1)} %collective-permute-done.2.refs_2_, ...), custom_call_target="tpu_custom_call" | custom-call | flops 8000000000 | bytes 6225920 | tf_op jit(solution)/shard_map/weights/pallas_call | solution.py:180
  60.0 8.8 %text_terms.1 = (f32[144,1280]{1,0:T(8,128)S(1)}, f32[160,1280]{1,0:T(8,128)S(1)}, bf16[144,1280]{1,0:T(8,128)(2,1)S(1)}, bf16[160,1280]{1,0:T(8,128)(2,1)S(1)},...) custom-call(s32[8]{0:T(128)S(1)} %stack.41.place, ...), custom_call_target="tpu_custom_call" | custom-call | flops 7549747200 | bytes 6553600 | tf_op jit(solution)/shard_map/text_terms/pallas_call | solution.py:224
  68.7 1.8 %collective-permute-start.23 = (bf16[144,1280]{1,0:T(8,128)(2,1)S(1)}, bf16[144,1280]{1,0:T(8,128)(2,1)S(1)}, u32[]{:S(2)}, u32[]{:S(2)}) collective-permute-start(bf16[144,1280]{1,0:T(8,128)(2,1)S(1)} %get-tuple-element.107), channel_id=1, source_target_pairs={{0,32},{1,33},{16,48},{17,49},{2,34},{3,35},{18,50},{19,51},{4,36}... | collective-permute-start | bytes 1105928 | tf_op jit(solution)/shard_map/ppermute | solution.py:56
  70.8 2.9 %collective-permute-start.33 = (bf16[160,1280]{1,0:T(8,128)(2,1)S(1)}, bf16[160,1280]{1,0:T(8,128)(2,1)S(1)}, u32[]{:S(2)}, u32[]{:S(2)}) collective-permute-start(bf16[160,1280]{1,0:T(8,128)(2,1)S(1)} %get-tuple-element.128), channel_id=1, source_target_pairs={{0,32},{1,33},{16,48},{17,49},{2,34},{3,35},{18,50},{19,51},{4,36}... | collective-permute-start | bytes 1228808 | tf_op jit(solution)/shard_map/ppermute | solution.py:56
  73.8 8.6 %image_terms.1 = (f32[160,1152]{1,0:T(8,128)S(1)}, f32[160,1152]{1,0:T(8,128)S(1)}, bf16[160,1152]{1,0:T(8,128)(2,1)S(1)}, bf16[160,1152]{1,0:T(8,128)(2,1)S(1)}...) custom-call(bf16[1280,1280]{1,0:T(8,128)(2,1)S(1)} %get-tuple-elemen, ...), custom_call_target="tpu_custom_call" | custom-call | flops 10000000000 | bytes 11796480 | tf_op jit(solution)/shard_map/image_terms/pallas_call | solution.py:254
  83.3 2.0 %collective-permute-start.24 = (bf16[160,1152]{1,0:T(8,128)(2,1)S(1)}, bf16[160,1152]{1,0:T(8,128)(2,1)S(1)}, u32[]{:S(2)}, u32[]{:S(2)}) collective-permute-start(bf16[160,1152]{1,0:T(8,128)(2,1)S(1)} %get-tuple-element.113), channel_id=1, source_target_pairs={{0,4},{1,5},{16,20},{17,21},{2,6},{3,7},{18,22},{19,23},{4,8},{5,9... | collective-permute-start | bytes 1105928 | tf_op jit(solution)/shard_map/ppermute | solution.py:56
  85.3 1.9 %collective-permute-start.34 = (bf16[160,1280]{1,0:T(8,128)(2,1)S(1)}, bf16[160,1280]{1,0:T(8,128)(2,1)S(1)}, u32[]{:S(2)}, u32[]{:S(2)}) collective-permute-start(bf16[160,1280]{1,0:T(8,128)(2,1)S(1)} %add_rows.4), channel_id=1, source_target_pairs={{0,96},{1,97},{16,112},{17,113},{2,98},{3,99},{18,114},{19,115},{4... | collective-permute-start | bytes 1228808 | tf_op jit(solution)/shard_map/ppermute | solution.py:56
  87.3 5.2 %collective-permute-done.27.refs_1_ = bf16[160,1152]{1,0:T(8,128)(2,1)S(1)} collective-permute-done((bf16[160,1152]{1,0:T(8,128)(2,1)S(1)}, bf16[160,1152]{1,0:T(8,128)(2,1)S(1)}, u32[]{:S(2)}, u32[]{:S(2)}) %collective-permute-start.27) | collective-permute-done | bytes 368672 | tf_op jit(solution)/shard_map/ppermute | solution.py:56
  93.4 2.5 %collective-permute-start.29 = (bf16[160,1152]{1,0:T(8,128)(2,1)S(1)}, bf16[160,1152]{1,0:T(8,128)(2,1)S(1)}, u32[]{:S(2)}, u32[]{:S(2)}) collective-permute-start(bf16[160,1152]{1,0:T(8,128)(2,1)S(1)} %add_rows.7), channel_id=1, source_target_pairs={{0,12},{1,13},{16,28},{17,29},{2,14},{3,15},{18,30},{19,31},{4,0},... | collective-permute-start | bytes 1105928 | tf_op jit(solution)/shard_map/ppermute | solution.py:56
  96.5 1.1 collective-permute-start.35
  98.2 4.2 %collective-permute-done.28.ahead = bf16[160,1152]{1,0:T(8,128)(2,1)S(1)} collective-permute-done((bf16[160,1152]{1,0:T(8,128)(2,1)S(1)}, bf16[160,1152]{1,0:T(8,128)(2,1)S(1)}, u32[]{:S(2)}, u32[]{:S(2)}) %collective-permute-start.28) | collective-permute-done | bytes 368672 | tf_op jit(solution)/shard_map/ppermute | solution.py:56
  102.5 2.7 %collective-permute-start.30 = (bf16[160,1152]{1,0:T(8,128)(2,1)S(1)}, bf16[160,1152]{1,0:T(8,128)(2,1)S(1)}, u32[]{:S(2)}, u32[]{:S(2)}) collective-permute-start(bf16[160,1152]{1,0:T(8,128)(2,1)S(1)} %add_three.2), channel_id=1, source_target_pairs={{0,2},{1,3},{16,18},{17,19},{2,0},{3,1},{18,16},{19,17},{4,6},{5,7... | collective-permute-start | bytes 1105928 | tf_op jit(solution)/shard_map/ppermute | solution.py:56
  105.2 3.2 %collective-permute-start.26 = (bf16[160,1152]{1,0:T(8,128)(2,1)S(1)}, bf16[160,1152]{1,0:T(8,128)(2,1)S(1)}, u32[]{:S(2)}, u32[]{:S(2)}) collective-permute-start(bf16[160,1152]{1,0:T(8,128)(2,1)S(1)} %get-tuple-element.116), channel_id=1, source_target_pairs={{0,12},{1,13},{16,28},{17,29},{2,14},{3,15},{18,30},{19,31},{4,0},... | collective-permute-start | bytes 1105928 | tf_op jit(solution)/shard_map/ppermute | solution.py:56
  108.4 1.1 text_final.1
  109.5 4.7 %collective-permute-done.30.given = bf16[160,1152]{1,0:T(8,128)(2,1)S(1)} collective-permute-done((bf16[160,1152]{1,0:T(8,128)(2,1)S(1)}, bf16[160,1152]{1,0:T(8,128)(2,1)S(1)}, u32[]{:S(2)}, u32[]{:S(2)}) %collective-permute-start.30) | collective-permute-done | bytes 368672 | tf_op jit(solution)/shard_map/ppermute | solution.py:56
  114.2 1.1 image_final.1
  (76 shorter events, 12.5 us)
Async XLA Ops:
  0.6 10.8 %collective-permute-start.1 = (bf16[144,1280]{1,0:T(8,128)(2,1)}, bf16[144,1280]{1,0:T(8,128)(2,1)S(1)}, u32[]{:S(2)}, u32[]{:S(2)}) collective-permute-start(bf16[144,1280]{1,0:T(8,128)(2,1)} %bitcast.12), channel_id=1, source_target_pairs={{0,16},{1,17},{16,0},{17,1},{2,18},{3,19},{18,2},{19,3},{4,20},{5,... | collective-permute-start | bytes 1105928 | tf_op jit(solution)/shard_map/ppermute | solution.py:56
  2.6 14.9 %collective-permute-start.11 = (bf16[144,1280]{1,0:T(8,128)(2,1)}, bf16[144,1280]{1,0:T(8,128)(2,1)S(1)}, u32[]{:S(2)}, u32[]{:S(2)}) collective-permute-start(bf16[144,1280]{1,0:T(8,128)(2,1)} %bitcast.13), channel_id=1, source_target_pairs={{0,96},{1,97},{16,112},{17,113},{2,98},{3,99},{18,114},{19,115},{4... | collective-permute-start | bytes 1105928 | tf_op jit(solution)/shard_map/ppermute | solution.py:56
  3.5 14.1 %collective-permute-start.9 = (bf16[144,1280]{1,0:T(8,128)(2,1)}, bf16[144,1280]{1,0:T(8,128)(2,1)S(1)}, u32[]{:S(2)}, u32[]{:S(2)}) collective-permute-start(bf16[144,1280]{1,0:T(8,128)(2,1)} %bitcast.14), channel_id=1, source_target_pairs={{0,32},{1,33},{16,48},{17,49},{2,34},{3,35},{18,50},{19,51},{4,36}... | collective-permute-start | bytes 1105928 | tf_op jit(solution)/shard_map/ppermute | solution.py:56
  7.7 11.9 %collective-permute-start.3 = (bf16[176,1152]{1,0:T(8,128)(2,1)S(1)}, bf16[176,1152]{1,0:T(8,128)(2,1)S(1)}, u32[]{:S(2)}, u32[]{:S(2)}) collective-permute-start(bf16[176,1152]{1,0:T(8,128)(2,1)S(1)} %get-tuple-element.68.value.refs_2_), channel_id=1, source_target_pairs={{0,12},{1,13},{16,28},{17,29},{2,14},{3,15},{18,30},{19,31},{4,0},... | collective-permute-start | bytes 1216520 | tf_op jit(solution)/shard_map/ppermute | solution.py:56
  10.8 11.9 %collective-permute-start = (bf16[176,1152]{1,0:T(8,128)(2,1)S(1)}, bf16[176,1152]{1,0:T(8,128)(2,1)S(1)}, u32[]{:S(2)}, u32[]{:S(2)}) collective-permute-start(bf16[176,1152]{1,0:T(8,128)(2,1)S(1)} %get-tuple-element.68.value.refs_2_), channel_id=1, source_target_pairs={{0,4},{1,5},{16,20},{17,21},{2,6},{3,7},{18,22},{19,23},{4,8},{5,9... | collective-permute-start | bytes 1216520 | tf_op jit(solution)/shard_map/ppermute | solution.py:56
  11.5 12.3 %collective-permute-start.2 = (bf16[176,1152]{1,0:T(8,128)(2,1)S(1)}, bf16[176,1152]{1,0:T(8,128)(2,1)S(1)}, u32[]{:S(2)}, u32[]{:S(2)}) collective-permute-start(bf16[176,1152]{1,0:T(8,128)(2,1)S(1)} %hold.1), channel_id=1, source_target_pairs={{0,2},{1,3},{16,18},{17,19},{2,0},{3,1},{18,16},{19,17},{4,6},{5,7... | collective-permute-start | bytes 1216520 | tf_op jit(solution)/shard_map/ppermute | solution.py:56
  17.5 15.8 %collective-permute-start.10 = (bf16[144,1280]{1,0:T(8,128)(2,1)S(1)}, bf16[144,1280]{1,0:T(8,128)(2,1)S(1)}, u32[]{:S(2)}, u32[]{:S(2)}) collective-permute-start(bf16[144,1280]{1,0:T(8,128)(2,1)S(1)} %collective-permute-done.1.refs_0_.refs_1_), channel_id=1, source_target_pairs={{0,32},{1,33},{16,48},{17,49},{2,34},{3,35},{18,50},{19,51},{4,36}... | collective-permute-start | bytes 1105928 | tf_op jit(solution)/shard_map/ppermute | solution.py:56
  18.0 14.3 %collective-permute-start.12 = (bf16[144,1280]{1,0:T(8,128)(2,1)S(1)}, bf16[144,1280]{1,0:T(8,128)(2,1)S(1)}, u32[]{:S(2)}, u32[]{:S(2)}) collective-permute-start(bf16[144,1280]{1,0:T(8,128)(2,1)S(1)} %collective-permute-done.1.refs_0_.refs_1_), channel_id=1, source_target_pairs={{0,96},{1,97},{16,112},{17,113},{2,98},{3,99},{18,114},{19,115},{4... | collective-permute-start | bytes 1105928 | tf_op jit(solution)/shard_map/ppermute | solution.py:56
  19.6 11.0 %collective-permute-start.5 = (bf16[80,1152]{1,0:T(8,128)(2,1)S(1)}, bf16[80,1152]{1,0:T(8,128)(2,1)S(1)}, u32[]{:S(2)}, u32[]{:S(2)}) collective-permute-start(bf16[80,1152]{1,0:T(8,128)(2,1)S(1)} %slice.17), channel_id=1, source_target_pairs={{0,12},{1,13},{16,28},{17,29},{2,14},{3,15},{18,30},{19,31},{4,0},... | collective-permute-start | bytes 552968 | tf_op jit(solution)/shard_map/ppermute | solution.py:56
  23.7 15.7 %collective-permute-start.8 = (bf16[176,1152]{1,0:T(8,128)(2,1)S(1)}, bf16[176,1152]{1,0:T(8,128)(2,1)S(1)}, u32[]{:S(2)}, u32[]{:S(2)}) collective-permute-start(bf16[176,1152]{1,0:T(8,128)(2,1)S(1)} %collective-permute-done.2.refs_2_), channel_id=1, source_target_pairs={{0,12},{1,13},{16,28},{17,29},{2,14},{3,15},{18,30},{19,31},{4,0},... | collective-permute-start | bytes 1216520 | tf_op jit(solution)/shard_map/ppermute | solution.py:56
  29.9 9.5 %collective-permute-start.7 = (bf16[176,1152]{1,0:T(8,128)(2,1)S(1)}, bf16[176,1152]{1,0:T(8,128)(2,1)S(1)}, u32[]{:S(2)}, u32[]{:S(2)}) collective-permute-start(bf16[176,1152]{1,0:T(8,128)(2,1)S(1)} %collective-permute-done.2.refs_2_), channel_id=1, source_target_pairs={{0,4},{1,5},{16,20},{17,21},{2,6},{3,7},{18,22},{19,23},{4,8},{5,9... | collective-permute-start | bytes 1216520 | tf_op jit(solution)/shard_map/ppermute | solution.py:56
  30.6 11.1 %collective-permute-start.15 = (bf16[144,1280]{1,0:T(8,128)(2,1)S(1)}, bf16[144,1280]{1,0:T(8,128)(2,1)S(1)}, u32[]{:S(2)}, u32[]{:S(2)}) collective-permute-start(bf16[144,1280]{1,0:T(8,128)(2,1)S(1)} %collective-permute-done.9.refs_2_), channel_id=1, source_target_pairs={{0,32},{1,33},{16,48},{17,49},{2,34},{3,35},{18,50},{19,51},{4,36}... | collective-permute-start | bytes 1105928 | tf_op jit(solution)/shard_map/ppermute | solution.py:56
  32.3 9.5 %collective-permute-start.16 = (bf16[144,1280]{1,0:T(8,128)(2,1)S(1)}, bf16[144,1280]{1,0:T(8,128)(2,1)S(1)}, u32[]{:S(2)}, u32[]{:S(2)}) collective-permute-start(bf16[144,1280]{1,0:T(8,128)(2,1)S(1)} %collective-permute-done.12.refs_5_), channel_id=1, source_target_pairs={{0,96},{1,97},{16,112},{17,113},{2,98},{3,99},{18,114},{19,115},{4... | collective-permute-start | bytes 1105928 | tf_op jit(solution)/shard_map/ppermute | solution.py:56
  33.4 13.7 %collective-permute-start.6 = (bf16[704,1152]{1,0:T(8,128)(2,1)}, bf16[704,1152]{1,0:T(8,128)(2,1)S(1)}, u32[]{:S(2)}, u32[]{:S(2)}) collective-permute-start(bf16[704,1152]{1,0:T(8,128)(2,1)} %constant_dynamic-update-slice_fusion), channel_id=1, source_target_pairs={{0,1},{1,0},{16,17},{17,16},{2,3},{3,2},{18,19},{19,18},{4,5},{5,4... | collective-permute-start | bytes 4866056 | tf_op jit(solution)/shard_map/ppermute | solution.py:56
  41.7 11.3 %collective-permute-start.18 = (bf16[528,1152]{1,0:T(8,128)(2,1)S(1)}, bf16[528,1152]{1,0:T(8,128)(2,1)S(1)}, u32[]{:S(2)}, u32[]{:S(2)}) collective-permute-start(bf16[528,1152]{1,0:T(8,128)(2,1)S(1)} %pad_maximum_fusion), channel_id=1, source_target_pairs={{0,1},{1,0},{16,17},{17,16},{2,3},{3,2},{18,19},{19,18},{4,5},{5,4... | collective-permute-start | bytes 3649544 | tf_op jit(solution)/shard_map/ppermute | solution.py:56
  58.9 14.9 %collective-permute-start.21 = (bf16[1152,1280]{1,0:T(8,128)(2,1)S(1)}, bf16[1152,1280]{1,0:T(8,128)(2,1)S(1)}, u32[]{:S(2)}, u32[]{:S(2)}) collective-permute-start(bf16[1152,1280]{1,0:T(8,128)(2,1)S(1)} %get-tuple-element.98.refs_8_.refs_9_.refs_4_), channel_id=1, source_target_pairs={{0,1},{1,0},{16,17},{17,16},{2,3},{3,2},{18,19},{19,18},{4,5},{5,4... | collective-permute-start | bytes 8847368 | tf_op jit(solution)/shard_map/ppermute | solution.py:56
  59.5 9.3 %collective-permute-start.20 = (bf16[640,1280]{1,0:T(8,128)(2,1)S(1)}, bf16[640,1280]{1,0:T(8,128)(2,1)S(1)}, u32[]{:S(2)}, u32[]{:S(2)}) collective-permute-start(bf16[640,1280]{1,0:T(8,128)(2,1)S(1)} %get-tuple-element.85), channel_id=1, source_target_pairs={{0,1},{1,0},{16,17},{17,16},{2,3},{3,2},{18,19},{19,18},{4,5},{5,4... | collective-permute-start | bytes 4915208 | tf_op jit(solution)/shard_map/ppermute | solution.py:56
  59.6 14.2 %collective-permute-start.17 = (bf16[640,1280]{1,0:T(8,128)(2,1)S(1)}, bf16[640,1280]{1,0:T(8,128)(2,1)S(1)}, u32[]{:S(2)}, u32[]{:S(2)}) collective-permute-start(bf16[640,1280]{1,0:T(8,128)(2,1)S(1)} %get-tuple-element.82), channel_id=1, source_target_pairs={{0,1},{1,0},{16,17},{17,16},{2,3},{3,2},{18,19},{19,18},{4,5},{5,4... | collective-permute-start | bytes 4915208 | tf_op jit(solution)/shard_map/ppermute | solution.py:56
  68.7 14.4 %collective-permute-start.23 = (bf16[144,1280]{1,0:T(8,128)(2,1)S(1)}, bf16[144,1280]{1,0:T(8,128)(2,1)S(1)}, u32[]{:S(2)}, u32[]{:S(2)}) collective-permute-start(bf16[144,1280]{1,0:T(8,128)(2,1)S(1)} %get-tuple-element.107), channel_id=1, source_target_pairs={{0,32},{1,33},{16,48},{17,49},{2,34},{3,35},{18,50},{19,51},{4,36}... | collective-permute-start | bytes 1105928 | tf_op jit(solution)/shard_map/ppermute | solution.py:56
  70.5 12.4 %collective-permute-start.22 = (bf16[160,1280]{1,0:T(8,128)(2,1)S(1)}, bf16[160,1280]{1,0:T(8,128)(2,1)S(1)}, u32[]{:S(2)}, u32[]{:S(2)}) collective-permute-start(bf16[160,1280]{1,0:T(8,128)(2,1)S(1)} %get-tuple-element.104), channel_id=1, source_target_pairs={{0,96},{1,97},{16,112},{17,113},{2,98},{3,99},{18,114},{19,115},{4... | collective-permute-start | bytes 1228808 | tf_op jit(solution)/shard_map/ppermute | solution.py:56
  70.8 22.5 %collective-permute-start.33 = (bf16[160,1280]{1,0:T(8,128)(2,1)S(1)}, bf16[160,1280]{1,0:T(8,128)(2,1)S(1)}, u32[]{:S(2)}, u32[]{:S(2)}) collective-permute-start(bf16[160,1280]{1,0:T(8,128)(2,1)S(1)} %get-tuple-element.128), channel_id=1, source_target_pairs={{0,32},{1,33},{16,48},{17,49},{2,34},{3,35},{18,50},{19,51},{4,36}... | collective-permute-start | bytes 1228808 | tf_op jit(solution)/shard_map/ppermute | solution.py:56
  83.0 9.5 %collective-permute-start.27 = (bf16[160,1152]{1,0:T(8,128)(2,1)S(1)}, bf16[160,1152]{1,0:T(8,128)(2,1)S(1)}, u32[]{:S(2)}, u32[]{:S(2)}) collective-permute-start(bf16[160,1152]{1,0:T(8,128)(2,1)S(1)} %get-tuple-element.119), channel_id=1, source_target_pairs={{0,12},{1,13},{16,28},{17,29},{2,14},{3,15},{18,30},{19,31},{4,0},... | collective-permute-start | bytes 1105928 | tf_op jit(solution)/shard_map/ppermute | solution.py:56
  83.2 22.0 %collective-permute-start.31 = (bf16[144,1280]{1,0:T(8,128)(2,1)S(1)}, bf16[144,1280]{1,0:T(8,128)(2,1)S(1)}, u32[]{:S(2)}, u32[]{:S(2)}) collective-permute-start(bf16[144,1280]{1,0:T(8,128)(2,1)S(1)} %add_rows.5), channel_id=1, source_target_pairs={{0,32},{1,33},{16,48},{17,49},{2,34},{3,35},{18,50},{19,51},{4,36}... | collective-permute-start | bytes 1105928 | tf_op jit(solution)/shard_map/ppermute | solution.py:56
  83.3 14.2 %collective-permute-start.24 = (bf16[160,1152]{1,0:T(8,128)(2,1)S(1)}, bf16[160,1152]{1,0:T(8,128)(2,1)S(1)}, u32[]{:S(2)}, u32[]{:S(2)}) collective-permute-start(bf16[160,1152]{1,0:T(8,128)(2,1)S(1)} %get-tuple-element.113), channel_id=1, source_target_pairs={{0,4},{1,5},{16,20},{17,21},{2,6},{3,7},{18,22},{19,23},{4,8},{5,9... | collective-permute-start | bytes 1105928 | tf_op jit(solution)/shard_map/ppermute | solution.py:56
  85.3 11.0 %collective-permute-start.34 = (bf16[160,1280]{1,0:T(8,128)(2,1)S(1)}, bf16[160,1280]{1,0:T(8,128)(2,1)S(1)}, u32[]{:S(2)}, u32[]{:S(2)}) collective-permute-start(bf16[160,1280]{1,0:T(8,128)(2,1)S(1)} %add_rows.4), channel_id=1, source_target_pairs={{0,96},{1,97},{16,112},{17,113},{2,98},{3,99},{18,114},{19,115},{4... | collective-permute-start | bytes 1228808 | tf_op jit(solution)/shard_map/ppermute | solution.py:56
  92.6 9.8 %collective-permute-start.28 = (bf16[160,1152]{1,0:T(8,128)(2,1)S(1)}, bf16[160,1152]{1,0:T(8,128)(2,1)S(1)}, u32[]{:S(2)}, u32[]{:S(2)}) collective-permute-start(bf16[160,1152]{1,0:T(8,128)(2,1)S(1)} %get-tuple-element.122), channel_id=1, source_target_pairs={{0,4},{1,5},{16,20},{17,21},{2,6},{3,7},{18,22},{19,23},{4,8},{5,9... | collective-permute-start | bytes 1105928 | tf_op jit(solution)/shard_map/ppermute | solution.py:56
  93.4 9.0 %collective-permute-start.29 = (bf16[160,1152]{1,0:T(8,128)(2,1)S(1)}, bf16[160,1152]{1,0:T(8,128)(2,1)S(1)}, u32[]{:S(2)}, u32[]{:S(2)}) collective-permute-start(bf16[160,1152]{1,0:T(8,128)(2,1)S(1)} %add_rows.7), channel_id=1, source_target_pairs={{0,12},{1,13},{16,28},{17,29},{2,14},{3,15},{18,30},{19,31},{4,0},... | collective-permute-start | bytes 1105928 | tf_op jit(solution)/shard_map/ppermute | solution.py:56
  96.5 12.0 %collective-permute-start.35 = (bf16[160,1280]{1,0:T(8,128)(2,1)S(1)}, bf16[160,1280]{1,0:T(8,128)(2,1)S(1)}, u32[]{:S(2)}, u32[]{:S(2)}) collective-permute-start(bf16[160,1280]{1,0:T(8,128)(2,1)S(1)} %add_three.3.gave), channel_id=1, source_target_pairs={{0,16},{1,17},{16,0},{17,1},{2,18},{3,19},{18,2},{19,3},{4,20},{5,... | collective-permute-start | bytes 1228808 | tf_op jit(solution)/shard_map/ppermute | solution.py:56
  97.6 10.8 %collective-permute-start.32 = (bf16[144,1280]{1,0:T(8,128)(2,1)S(1)}, bf16[144,1280]{1,0:T(8,128)(2,1)S(1)}, u32[]{:S(2)}, u32[]{:S(2)}) collective-permute-start(bf16[144,1280]{1,0:T(8,128)(2,1)S(1)} %get-tuple-element.126), channel_id=1, source_target_pairs={{0,96},{1,97},{16,112},{17,113},{2,98},{3,99},{18,114},{19,115},{4... | collective-permute-start | bytes 1105928 | tf_op jit(solution)/shard_map/ppermute | solution.py:56
  102.5 11.7 %collective-permute-start.30 = (bf16[160,1152]{1,0:T(8,128)(2,1)S(1)}, bf16[160,1152]{1,0:T(8,128)(2,1)S(1)}, u32[]{:S(2)}, u32[]{:S(2)}) collective-permute-start(bf16[160,1152]{1,0:T(8,128)(2,1)S(1)} %add_three.2), channel_id=1, source_target_pairs={{0,2},{1,3},{16,18},{17,19},{2,0},{3,1},{18,16},{19,17},{4,6},{5,7... | collective-permute-start | bytes 1105928 | tf_op jit(solution)/shard_map/ppermute | solution.py:56
  105.2 9.0 %collective-permute-start.25 = (bf16[160,1152]{1,0:T(8,128)(2,1)S(1)}, bf16[160,1152]{1,0:T(8,128)(2,1)S(1)}, u32[]{:S(2)}, u32[]{:S(2)}) collective-permute-start(bf16[160,1152]{1,0:T(8,128)(2,1)S(1)} %add_rows.6), channel_id=1, source_target_pairs={{0,4},{1,5},{16,20},{17,21},{2,6},{3,7},{18,22},{19,23},{4,8},{5,9... | collective-permute-start | bytes 1105928 | tf_op jit(solution)/shard_map/ppermute | solution.py:56
  105.2 9.0 %collective-permute-start.26 = (bf16[160,1152]{1,0:T(8,128)(2,1)S(1)}, bf16[160,1152]{1,0:T(8,128)(2,1)S(1)}, u32[]{:S(2)}, u32[]{:S(2)}) collective-permute-start(bf16[160,1152]{1,0:T(8,128)(2,1)S(1)} %get-tuple-element.116), channel_id=1, source_target_pairs={{0,12},{1,13},{16,28},{17,29},{2,14},{3,15},{18,30},{19,31},{4,0},... | collective-permute-start | bytes 1105928 | tf_op jit(solution)/shard_map/ppermute | solution.py:56
  (8 other events, 48.1 us)

commit v2 on v0

--- a/solution.py
+++ b/solution.py
@@ -156,8 +156,8 @@
     names = (lax.broadcasted_iota(jnp.int32, (rows, columns), 1) + first_text[0]).astype(F32)
 
     def step(number, carry):
-        for k in range(4):
-            block = number * 4 + k
+        for k in range(8):
+            block = number * 8 + k
             mine = pl.ds(pl.multiple_of(block * rows, 16), rows)
             tail = tails[pl.ds(pl.multiple_of(block * TAIL, 16), TAIL), :].astype(F32)
             product = lax.dot_general(
@@ -170,7 +170,7 @@
             weight[mine, :] = (chance - jnp.where(match == names, 1.0, 0.0)).astype(BF16)
         return carry
 
-    lax.fori_loop(0, 8 // 4, step, 0)
+    lax.fori_loop(0, 8 // 8, step, 0)
     other[...] = weight[4 * rows :, :]
 
 
@@ -197,15 +197,16 @@
     outs, back = refs[:8], refs[8]
     width, columns = back.shape
     block = 384
-    dots = jnp.zeros((1, columns), F32)
-    for f in range(0, width, block):
+
+    def step(number, dots):
+        mine = pl.ds(pl.multiple_of(number * block, block), block)
         part = lax.dot_general(
-            image_a[:, f : f + block], weight_a[...], TN, preferred_element_type=F32
-        ) + lax.dot_general(
-            image_b[:, f : f + block], weight_b[...], TN, preferred_element_type=F32
-        )
-        back[f : f + block, :] = part
-        dots += jnp.sum(part * raw[f : f + block, :].astype(F32), axis=0, keepdims=True)
+            image_a[:, mine], weight_a[...], TN, preferred_element_type=F32
+        ) + lax.dot_general(image_b[:, mine], weight_b[...], TN, preferred_element_type=F32)
+        back[mine, :] = part
+        return dots + jnp.sum(part * raw[mine, :].astype(F32), axis=0, keepdims=True)
+
+    dots = lax.fori_loop(0, width // block, step, jnp.zeros((1, columns), F32))
     tail = split3(dots)
     empty = jnp.zeros((1, columns), F32)
     depth = width // 8

time: 117 us -> 116 us (level)
  no operation moved by 1% of the time
where the time goes in v2:
time: 116 us
  starting transfers between devices  46.3 us (40%)
  Pallas kernels  33.6 us (29%)
  waiting for transfers between devices  28.3 us (24%)
  local copies, waits for them, and re-layouts  5.58 us (5%)
  between operations  2.23 us (2%)
    ppermute x36, starting transfers between devices, send(): return lax.ppermute(value, AXES, MOVES[move])  46.3 us
    ppermute x36, waiting for transfers between devices, send(): return lax.ppermute(value, AXES, MOVES[move])  28.3 us
    pallas_call x2, Pallas kernels, weights(): pl.pallas_call(lambda *refs: weight_kernel(rows, *refs), out_shape=[jax.S...  10.9 us
    pallas_call x1, Pallas kernels, text_terms(): pl.pallas_call(text_back_kernel, out_shape=[jax.ShapeDtypeStruct((width /...  9.27 us
    pallas_call x1, Pallas kernels, image_terms(): pl.pallas_call(lambda *refs: image_back_kernel(rows, *refs), out_shape=[j...  8.64 us
    unnamed x12, local copies, waits for them, and re-layouts  4.73 us
  transfers between devices with their start and end apart: 36, of which 10 were waited for; matrix products, arithmetic and copies ran while one was open for 4% of the time, Pallas kernels for 23%

profile of v2, /device:TPU:6, one launch (start us, length us, event | category | flops | bytes accessed | tf_op | source)
XLA Modules:
  0.0 116.2 jit_solution(4829254021015310210)
XLA Ops:
  0.6 2.0 %collective-permute-start.1 = (bf16[144,1280]{1,0:T(8,128)(2,1)}, bf16[144,1280]{1,0:T(8,128)(2,1)S(1)}, u32[]{:S(2)}, u32[]{:S(2)}) collective-permute-start(bf16[144,1280]{1,0:T(8,128)(2,1)} %bitcast.12), channel_id=1, source_target_pairs={{0,16},{1,17},{16,0},{17,1},{2,18},{3,19},{18,2},{19,3},{4,20},{5,... | collective-permute-start | bytes 1105928 | tf_op jit(solution)/shard_map/ppermute | solution.py:56
  3.5 2.4 %collective-permute-start.9 = (bf16[144,1280]{1,0:T(8,128)(2,1)}, bf16[144,1280]{1,0:T(8,128)(2,1)S(1)}, u32[]{:S(2)}, u32[]{:S(2)}) collective-permute-start(bf16[144,1280]{1,0:T(8,128)(2,1)} %bitcast.14), channel_id=1, source_target_pairs={{0,32},{1,33},{16,48},{17,49},{2,34},{3,35},{18,50},{19,51},{4,36}... | collective-permute-start | bytes 1105928 | tf_op jit(solution)/shard_map/ppermute | solution.py:56
  7.7 3.1 %collective-permute-start.3 = (bf16[176,1152]{1,0:T(8,128)(2,1)S(1)}, bf16[176,1152]{1,0:T(8,128)(2,1)S(1)}, u32[]{:S(2)}, u32[]{:S(2)}) collective-permute-start(bf16[176,1152]{1,0:T(8,128)(2,1)S(1)} %get-tuple-element.66.value.refs_2_), channel_id=1, source_target_pairs={{0,12},{1,13},{16,28},{17,29},{2,14},{3,15},{18,30},{19,31},{4,0},... | collective-permute-start | bytes 1216520 | tf_op jit(solution)/shard_map/ppermute | solution.py:56
  11.5 3.8 %collective-permute-start.2 = (bf16[176,1152]{1,0:T(8,128)(2,1)S(1)}, bf16[176,1152]{1,0:T(8,128)(2,1)S(1)}, u32[]{:S(2)}, u32[]{:S(2)}) collective-permute-start(bf16[176,1152]{1,0:T(8,128)(2,1)S(1)} %hold.1), channel_id=1, source_target_pairs={{0,2},{1,3},{16,18},{17,19},{2,0},{3,1},{18,16},{19,17},{4,6},{5,7... | collective-permute-start | bytes 1216520 | tf_op jit(solution)/shard_map/ppermute | solution.py:56
  18.0 1.5 %collective-permute-start.12 = (bf16[144,1280]{1,0:T(8,128)(2,1)S(1)}, bf16[144,1280]{1,0:T(8,128)(2,1)S(1)}, u32[]{:S(2)}, u32[]{:S(2)}) collective-permute-start(bf16[144,1280]{1,0:T(8,128)(2,1)S(1)} %collective-permute-done.1.refs_0_.refs_1_), channel_id=1, source_target_pairs={{0,96},{1,97},{16,112},{17,113},{2,98},{3,99},{18,114},{19,115},{4... | collective-permute-start | bytes 1105928 | tf_op jit(solution)/shard_map/ppermute | solution.py:56
  19.6 3.1 %collective-permute-start.5 = (bf16[80,1152]{1,0:T(8,128)(2,1)S(1)}, bf16[80,1152]{1,0:T(8,128)(2,1)S(1)}, u32[]{:S(2)}, u32[]{:S(2)}) collective-permute-start(bf16[80,1152]{1,0:T(8,128)(2,1)S(1)} %slice.17), channel_id=1, source_target_pairs={{0,12},{1,13},{16,28},{17,29},{2,14},{3,15},{18,30},{19,31},{4,0},... | collective-permute-start | bytes 552968 | tf_op jit(solution)/shard_map/ppermute | solution.py:56
  23.7 3.1 %collective-permute-start.8 = (bf16[176,1152]{1,0:T(8,128)(2,1)S(1)}, bf16[176,1152]{1,0:T(8,128)(2,1)S(1)}, u32[]{:S(2)}, u32[]{:S(2)}) collective-permute-start(bf16[176,1152]{1,0:T(8,128)(2,1)S(1)} %collective-permute-done.2.refs_2_), channel_id=1, source_target_pairs={{0,12},{1,13},{16,28},{17,29},{2,14},{3,15},{18,30},{19,31},{4,0},... | collective-permute-start | bytes 1216520 | tf_op jit(solution)/shard_map/ppermute | solution.py:56
  27.6 2.3 %collective-permute-done.4.refs_5_ = bf16[96,1152]{1,0:T(8,128)(2,1)S(1)} collective-permute-done((bf16[96,1152]{1,0:T(8,128)(2,1)S(1)}, bf16[96,1152]{1,0:T(8,128)(2,1)S(1)}, u32[]{:S(2)}, u32[]{:S(2)}) %collective-permute-start.4) | collective-permute-done | bytes 221216 | tf_op jit(solution)/shard_map/ppermute | solution.py:56
  30.6 1.7 %collective-permute-start.15 = (bf16[144,1280]{1,0:T(8,128)(2,1)S(1)}, bf16[144,1280]{1,0:T(8,128)(2,1)S(1)}, u32[]{:S(2)}, u32[]{:S(2)}) collective-permute-start(bf16[144,1280]{1,0:T(8,128)(2,1)S(1)} %collective-permute-done.9.refs_2_), channel_id=1, source_target_pairs={{0,32},{1,33},{16,48},{17,49},{2,34},{3,35},{18,50},{19,51},{4,36}... | collective-permute-start | bytes 1105928 | tf_op jit(solution)/shard_map/ppermute | solution.py:56
  33.4 6.0 %collective-permute-done.7.refs_3_ = bf16[176,1152]{1,0:T(8,128)(2,1)S(1)} collective-permute-done((bf16[176,1152]{1,0:T(8,128)(2,1)S(1)}, bf16[176,1152]{1,0:T(8,128)(2,1)S(1)}, u32[]{:S(2)}, u32[]{:S(2)}) %collective-permute-start.7) | collective-permute-done | bytes 405536 | tf_op jit(solution)/shard_map/ppermute | solution.py:56
  39.5 2.1 %collective-permute-start.13 = (bf16[96,1152]{1,0:T(8,128)(2,1)S(1)}, bf16[96,1152]{1,0:T(8,128)(2,1)S(1)}, u32[]{:S(2)}, u32[]{:S(2)}) collective-permute-start(bf16[96,1152]{1,0:T(8,128)(2,1)S(1)} %slice.14), channel_id=1, source_target_pairs={{0,4},{1,5},{16,20},{17,21},{2,6},{3,7},{18,22},{19,23},{4,8},{5,9... | collective-permute-start | bytes 663560 | tf_op jit(solution)/shard_map/ppermute | solution.py:56
  41.8 1.7 %text_units.1 = (bf16[1152,1280]{1,0:T(8,128)(2,1)S(1)}, bf16[1152,1280]{1,0:T(8,128)(2,1)S(1)}, f32[1,1280]{1,0:T(1,128)S(1)}) custom-call(s32[8]{0:T(128)S(1)} %stack.41.place, bf16[144,1280]{1,0:T(8,128)(2,1)S(1)} %bitcast.15, bf16[144,1280]{1,0:T(8,128)(2,1)S(1)} %collective-permute-done.1.refs_0_.refs_1_, ...), custom_call_target="tpu_custom_call" | custom-call | flops 40000000000 | bytes 5898240 | tf_op jit(solution)/shard_map/text_units/pallas_call | solution.py:125
  43.6 1.4 %collective-permute-done.14.refs_6_ = bf16[80,1152]{1,0:T(8,128)(2,1)S(1)} collective-permute-done((bf16[80,1152]{1,0:T(8,128)(2,1)S(1)}, bf16[80,1152]{1,0:T(8,128)(2,1)S(1)}, u32[]{:S(2)}, u32[]{:S(2)}) %collective-permute-start.14) | collective-permute-done | bytes 184352 | tf_op jit(solution)/shard_map/ppermute | solution.py:56
  45.0 1.7 %collective-permute-done.13.refs_5_ = bf16[96,1152]{1,0:T(8,128)(2,1)S(1)} collective-permute-done((bf16[96,1152]{1,0:T(8,128)(2,1)S(1)}, bf16[96,1152]{1,0:T(8,128)(2,1)S(1)}, u32[]{:S(2)}, u32[]{:S(2)}) %collective-permute-start.13) | collective-permute-done | bytes 221216 | tf_op jit(solution)/shard_map/ppermute | solution.py:56
  47.1 5.5 %weights.2 = (bf16[1280,1152]{1,0:T(8,128)(2,1)S(1)}, bf16[1280,1280]{1,0:T(8,128)(2,1)S(1)}, bf16[640,1280]{1,0:T(8,128)(2,1)S(1)}) custom-call(f32[2]{0:T(128)S(1)} %pad_maximum_fusion.2.refs_0_, s32[1]{0:T(128)} %bitcast.refs_1_, bf16[176,1152]{1,0:T(8,128)(2,1)S(1)} %get-tuple-element.66.value.refs_2_, ...), custom_call_target="tpu_custom_call" | custom-call | flops 8000000000 | bytes 6225920 | tf_op jit(solution)/shard_map/weights/pallas_call | solution.py:180
  52.6 5.5 %weights.3 = (bf16[1280,1152]{1,0:T(8,128)(2,1)S(1)}, bf16[1280,1280]{1,0:T(8,128)(2,1)S(1)}, bf16[640,1280]{1,0:T(8,128)(2,1)S(1)}) custom-call(f32[2]{0:T(128)S(1)} %pad_maximum_fusion.2.refs_0_, s32[1]{0:T(128)} %bitcast.refs_1_, bf16[176,1152]{1,0:T(8,128)(2,1)S(1)} %collective-permute-done.2.refs_2_, ...), custom_call_target="tpu_custom_call" | custom-call | flops 8000000000 | bytes 6225920 | tf_op jit(solution)/shard_map/weights/pallas_call | solution.py:180
  59.1 9.3 %text_terms.1 = (f32[144,1280]{1,0:T(8,128)S(1)}, f32[160,1280]{1,0:T(8,128)S(1)}, bf16[144,1280]{1,0:T(8,128)(2,1)S(1)}, bf16[160,1280]{1,0:T(8,128)(2,1)S(1)},...) custom-call(s32[8]{0:T(128)S(1)} %stack.41.place, ...), custom_call_target="tpu_custom_call" | custom-call | flops 7549747200 | bytes 6553600 | tf_op jit(solution)/shard_map/text_terms/pallas_call | solution.py:225
  68.4 2.0 %collective-permute-start.22 = (bf16[144,1280]{1,0:T(8,128)(2,1)S(1)}, bf16[144,1280]{1,0:T(8,128)(2,1)S(1)}, u32[]{:S(2)}, u32[]{:S(2)}) collective-permute-start(bf16[144,1280]{1,0:T(8,128)(2,1)S(1)} %get-tuple-element.102), channel_id=1, source_target_pairs={{0,32},{1,33},{16,48},{17,49},{2,34},{3,35},{18,50},{19,51},{4,36}... | collective-permute-start | bytes 1105928 | tf_op jit(solution)/shard_map/ppermute | solution.py:56
  70.5 1.9 %collective-permute-start.33 = (bf16[160,1280]{1,0:T(8,128)(2,1)S(1)}, bf16[160,1280]{1,0:T(8,128)(2,1)S(1)}, u32[]{:S(2)}, u32[]{:S(2)}) collective-permute-start(bf16[160,1280]{1,0:T(8,128)(2,1)S(1)} %get-tuple-element.125), channel_id=1, source_target_pairs={{0,96},{1,97},{16,112},{17,113},{2,98},{3,99},{18,114},{19,115},{4... | collective-permute-start | bytes 1228808 | tf_op jit(solution)/shard_map/ppermute | solution.py:56
  72.4 8.6 %image_terms.1 = (f32[160,1152]{1,0:T(8,128)S(1)}, f32[160,1152]{1,0:T(8,128)S(1)}, bf16[160,1152]{1,0:T(8,128)(2,1)S(1)}, bf16[160,1152]{1,0:T(8,128)(2,1)S(1)}...) custom-call(bf16[1280,1280]{1,0:T(8,128)(2,1)S(1)} %get-tuple-elemen, ...), custom_call_target="tpu_custom_call" | custom-call | flops 10000000000 | bytes 11796480 | tf_op jit(solution)/shard_map/image_terms/pallas_call | solution.py:255
  81.2 2.0 %collective-permute-start.30 = (bf16[144,1280]{1,0:T(8,128)(2,1)S(1)}, bf16[144,1280]{1,0:T(8,128)(2,1)S(1)}, u32[]{:S(2)}, u32[]{:S(2)}) collective-permute-start(bf16[144,1280]{1,0:T(8,128)(2,1)S(1)} %add_rows.4), channel_id=1, source_target_pairs={{0,32},{1,33},{16,48},{17,49},{2,34},{3,35},{18,50},{19,51},{4,36}... | collective-permute-start | bytes 1105928 | tf_op jit(solution)/shard_map/ppermute | solution.py:56
  83.9 2.5 %collective-permute-start.26 = (bf16[160,1152]{1,0:T(8,128)(2,1)S(1)}, bf16[160,1152]{1,0:T(8,128)(2,1)S(1)}, u32[]{:S(2)}, u32[]{:S(2)}) collective-permute-start(bf16[160,1152]{1,0:T(8,128)(2,1)S(1)} %get-tuple-element.114), channel_id=1, source_target_pairs={{0,12},{1,13},{16,28},{17,29},{2,14},{3,15},{18,30},{19,31},{4,0},... | collective-permute-start | bytes 1105928 | tf_op jit(solution)/shard_map/ppermute | solution.py:56
  86.7 6.1 %collective-permute-done.26.refs_1_ = bf16[160,1152]{1,0:T(8,128)(2,1)S(1)} collective-permute-done((bf16[160,1152]{1,0:T(8,128)(2,1)S(1)}, bf16[160,1152]{1,0:T(8,128)(2,1)S(1)}, u32[]{:S(2)}, u32[]{:S(2)}) %collective-permute-start.26) | collective-permute-done | bytes 368672 | tf_op jit(solution)/shard_map/ppermute | solution.py:56
  93.2 3.5 %collective-permute-start.28 = (bf16[160,1152]{1,0:T(8,128)(2,1)S(1)}, bf16[160,1152]{1,0:T(8,128)(2,1)S(1)}, u32[]{:S(2)}, u32[]{:S(2)}) collective-permute-start(bf16[160,1152]{1,0:T(8,128)(2,1)S(1)} %add_rows.6), channel_id=1, source_target_pairs={{0,12},{1,13},{16,28},{17,29},{2,14},{3,15},{18,30},{19,31},{4,0},... | collective-permute-start | bytes 1105928 | tf_op jit(solution)/shard_map/ppermute | solution.py:56
  97.4 1.1 collective-permute-start.35
  98.7 4.1 %collective-permute-done.27.ahead = bf16[160,1152]{1,0:T(8,128)(2,1)S(1)} collective-permute-done((bf16[160,1152]{1,0:T(8,128)(2,1)S(1)}, bf16[160,1152]{1,0:T(8,128)(2,1)S(1)}, u32[]{:S(2)}, u32[]{:S(2)}) %collective-permute-start.27) | collective-permute-done | bytes 368672 | tf_op jit(solution)/shard_map/ppermute | solution.py:56
  102.9 2.7 %collective-permute-start.29 = (bf16[160,1152]{1,0:T(8,128)(2,1)S(1)}, bf16[160,1152]{1,0:T(8,128)(2,1)S(1)}, u32[]{:S(2)}, u32[]{:S(2)}) collective-permute-start(bf16[160,1152]{1,0:T(8,128)(2,1)S(1)} %add_three.2), channel_id=1, source_target_pairs={{0,2},{1,3},{16,18},{17,19},{2,0},{3,1},{18,16},{19,17},{4,6},{5,7... | collective-permute-start | bytes 1105928 | tf_op jit(solution)/shard_map/ppermute | solution.py:56
  105.6 1.1 collective-permute-start.24
  106.7 2.1 %collective-permute-start.25 = (bf16[160,1152]{1,0:T(8,128)(2,1)S(1)}, bf16[160,1152]{1,0:T(8,128)(2,1)S(1)}, u32[]{:S(2)}, u32[]{:S(2)}) collective-permute-start(bf16[160,1152]{1,0:T(8,128)(2,1)S(1)} %get-tuple-element.111), channel_id=1, source_target_pairs={{0,12},{1,13},{16,28},{17,29},{2,14},{3,15},{18,30},{19,31},{4,0},... | collective-permute-start | bytes 1105928 | tf_op jit(solution)/shard_map/ppermute | solution.py:56
  108.8 1.1 text_final.1
  109.9 5.2 %collective-permute-done.29.given = bf16[160,1152]{1,0:T(8,128)(2,1)S(1)} collective-permute-done((bf16[160,1152]{1,0:T(8,128)(2,1)S(1)}, bf16[160,1152]{1,0:T(8,128)(2,1)S(1)}, u32[]{:S(2)}, u32[]{:S(2)}) %collective-permute-start.29) | collective-permute-done | bytes 368672 | tf_op jit(solution)/shard_map/ppermute | solution.py:56
  115.1 1.1 image_final.1
  (76 shorter events, 12.5 us)
Async XLA Ops:
  0.6 10.8 %collective-permute-start.1 = (bf16[144,1280]{1,0:T(8,128)(2,1)}, bf16[144,1280]{1,0:T(8,128)(2,1)S(1)}, u32[]{:S(2)}, u32[]{:S(2)}) collective-permute-start(bf16[144,1280]{1,0:T(8,128)(2,1)} %bitcast.12), channel_id=1, source_target_pairs={{0,16},{1,17},{16,0},{17,1},{2,18},{3,19},{18,2},{19,3},{4,20},{5,... | collective-permute-start | bytes 1105928 | tf_op jit(solution)/shard_map/ppermute | solution.py:56
  2.6 14.9 %collective-permute-start.11 = (bf16[144,1280]{1,0:T(8,128)(2,1)}, bf16[144,1280]{1,0:T(8,128)(2,1)S(1)}, u32[]{:S(2)}, u32[]{:S(2)}) collective-permute-start(bf16[144,1280]{1,0:T(8,128)(2,1)} %bitcast.13), channel_id=1, source_target_pairs={{0,96},{1,97},{16,112},{17,113},{2,98},{3,99},{18,114},{19,115},{4... | collective-permute-start | bytes 1105928 | tf_op jit(solution)/shard_map/ppermute | solution.py:56
  3.5 14.1 %collective-permute-start.9 = (bf16[144,1280]{1,0:T(8,128)(2,1)}, bf16[144,1280]{1,0:T(8,128)(2,1)S(1)}, u32[]{:S(2)}, u32[]{:S(2)}) collective-permute-start(bf16[144,1280]{1,0:T(8,128)(2,1)} %bitcast.14), channel_id=1, source_target_pairs={{0,32},{1,33},{16,48},{17,49},{2,34},{3,35},{18,50},{19,51},{4,36}... | collective-permute-start | bytes 1105928 | tf_op jit(solution)/shard_map/ppermute | solution.py:56
  7.7 11.9 %collective-permute-start.3 = (bf16[176,1152]{1,0:T(8,128)(2,1)S(1)}, bf16[176,1152]{1,0:T(8,128)(2,1)S(1)}, u32[]{:S(2)}, u32[]{:S(2)}) collective-permute-start(bf16[176,1152]{1,0:T(8,128)(2,1)S(1)} %get-tuple-element.66.value.refs_2_), channel_id=1, source_target_pairs={{0,12},{1,13},{16,28},{17,29},{2,14},{3,15},{18,30},{19,31},{4,0},... | collective-permute-start | bytes 1216520 | tf_op jit(solution)/shard_map/ppermute | solution.py:56
  10.8 11.9 %collective-permute-start = (bf16[176,1152]{1,0:T(8,128)(2,1)S(1)}, bf16[176,1152]{1,0:T(8,128)(2,1)S(1)}, u32[]{:S(2)}, u32[]{:S(2)}) collective-permute-start(bf16[176,1152]{1,0:T(8,128)(2,1)S(1)} %get-tuple-element.66.value.refs_2_), channel_id=1, source_target_pairs={{0,4},{1,5},{16,20},{17,21},{2,6},{3,7},{18,22},{19,23},{4,8},{5,9... | collective-permute-start | bytes 1216520 | tf_op jit(solution)/shard_map/ppermute | solution.py:56
  11.5 12.3 %collective-permute-start.2 = (bf16[176,1152]{1,0:T(8,128)(2,1)S(1)}, bf16[176,1152]{1,0:T(8,128)(2,1)S(1)}, u32[]{:S(2)}, u32[]{:S(2)}) collective-permute-start(bf16[176,1152]{1,0:T(8,128)(2,1)S(1)} %hold.1), channel_id=1, source_target_pairs={{0,2},{1,3},{16,18},{17,19},{2,0},{3,1},{18,16},{19,17},{4,6},{5,7... | collective-permute-start | bytes 1216520 | tf_op jit(solution)/shard_map/ppermute | solution.py:56
  17.5 15.8 %collective-permute-start.10 = (bf16[144,1280]{1,0:T(8,128)(2,1)S(1)}, bf16[144,1280]{1,0:T(8,128)(2,1)S(1)}, u32[]{:S(2)}, u32[]{:S(2)}) collective-permute-start(bf16[144,1280]{1,0:T(8,128)(2,1)S(1)} %collective-permute-done.1.refs_0_.refs_1_), channel_id=1, source_target_pairs={{0,32},{1,33},{16,48},{17,49},{2,34},{3,35},{18,50},{19,51},{4,36}... | collective-permute-start | bytes 1105928 | tf_op jit(solution)/shard_map/ppermute | solution.py:56
  18.0 14.3 %collective-permute-start.12 = (bf16[144,1280]{1,0:T(8,128)(2,1)S(1)}, bf16[144,1280]{1,0:T(8,128)(2,1)S(1)}, u32[]{:S(2)}, u32[]{:S(2)}) collective-permute-start(bf16[144,1280]{1,0:T(8,128)(2,1)S(1)} %collective-permute-done.1.refs_0_.refs_1_), channel_id=1, source_target_pairs={{0,96},{1,97},{16,112},{17,113},{2,98},{3,99},{18,114},{19,115},{4... | collective-permute-start | bytes 1105928 | tf_op jit(solution)/shard_map/ppermute | solution.py:56
  19.6 11.0 %collective-permute-start.5 = (bf16[80,1152]{1,0:T(8,128)(2,1)S(1)}, bf16[80,1152]{1,0:T(8,128)(2,1)S(1)}, u32[]{:S(2)}, u32[]{:S(2)}) collective-permute-start(bf16[80,1152]{1,0:T(8,128)(2,1)S(1)} %slice.17), channel_id=1, source_target_pairs={{0,12},{1,13},{16,28},{17,29},{2,14},{3,15},{18,30},{19,31},{4,0},... | collective-permute-start | bytes 552968 | tf_op jit(solution)/shard_map/ppermute | solution.py:56
  23.7 15.7 %collective-permute-start.8 = (bf16[176,1152]{1,0:T(8,128)(2,1)S(1)}, bf16[176,1152]{1,0:T(8,128)(2,1)S(1)}, u32[]{:S(2)}, u32[]{:S(2)}) collective-permute-start(bf16[176,1152]{1,0:T(8,128)(2,1)S(1)} %collective-permute-done.2.refs_2_), channel_id=1, source_target_pairs={{0,12},{1,13},{16,28},{17,29},{2,14},{3,15},{18,30},{19,31},{4,0},... | collective-permute-start | bytes 1216520 | tf_op jit(solution)/shard_map/ppermute | solution.py:56
  29.9 9.5 %collective-permute-start.7 = (bf16[176,1152]{1,0:T(8,128)(2,1)S(1)}, bf16[176,1152]{1,0:T(8,128)(2,1)S(1)}, u32[]{:S(2)}, u32[]{:S(2)}) collective-permute-start(bf16[176,1152]{1,0:T(8,128)(2,1)S(1)} %collective-permute-done.2.refs_2_), channel_id=1, source_target_pairs={{0,4},{1,5},{16,20},{17,21},{2,6},{3,7},{18,22},{19,23},{4,8},{5,9... | collective-permute-start | bytes 1216520 | tf_op jit(solution)/shard_map/ppermute | solution.py:56
  30.6 11.1 %collective-permute-start.15 = (bf16[144,1280]{1,0:T(8,128)(2,1)S(1)}, bf16[144,1280]{1,0:T(8,128)(2,1)S(1)}, u32[]{:S(2)}, u32[]{:S(2)}) collective-permute-start(bf16[144,1280]{1,0:T(8,128)(2,1)S(1)} %collective-permute-done.9.refs_2_), channel_id=1, source_target_pairs={{0,32},{1,33},{16,48},{17,49},{2,34},{3,35},{18,50},{19,51},{4,36}... | collective-permute-start | bytes 1105928 | tf_op jit(solution)/shard_map/ppermute | solution.py:56
  32.3 9.5 %collective-permute-start.16 = (bf16[144,1280]{1,0:T(8,128)(2,1)S(1)}, bf16[144,1280]{1,0:T(8,128)(2,1)S(1)}, u32[]{:S(2)}, u32[]{:S(2)}) collective-permute-start(bf16[144,1280]{1,0:T(8,128)(2,1)S(1)} %collective-permute-done.12.refs_5_), channel_id=1, source_target_pairs={{0,96},{1,97},{16,112},{17,113},{2,98},{3,99},{18,114},{19,115},{4... | collective-permute-start | bytes 1105928 | tf_op jit(solution)/shard_map/ppermute | solution.py:56
  33.4 13.7 %collective-permute-start.6 = (bf16[704,1152]{1,0:T(8,128)(2,1)}, bf16[704,1152]{1,0:T(8,128)(2,1)S(1)}, u32[]{:S(2)}, u32[]{:S(2)}) collective-permute-start(bf16[704,1152]{1,0:T(8,128)(2,1)} %constant_dynamic-update-slice_fusion), channel_id=1, source_target_pairs={{0,1},{1,0},{16,17},{17,16},{2,3},{3,2},{18,19},{19,18},{4,5},{5,4... | collective-permute-start | bytes 4866056 | tf_op jit(solution)/shard_map/ppermute | solution.py:56
  41.7 10.8 %collective-permute-start.18 = (bf16[528,1152]{1,0:T(8,128)(2,1)S(1)}, bf16[528,1152]{1,0:T(8,128)(2,1)S(1)}, u32[]{:S(2)}, u32[]{:S(2)}) collective-permute-start(bf16[528,1152]{1,0:T(8,128)(2,1)S(1)} %pad_maximum_fusion), channel_id=1, source_target_pairs={{0,1},{1,0},{16,17},{17,16},{2,3},{3,2},{18,19},{19,18},{4,5},{5,4... | collective-permute-start | bytes 3649544 | tf_op jit(solution)/shard_map/ppermute | solution.py:56
  58.0 14.4 %collective-permute-start.21 = (bf16[1152,1280]{1,0:T(8,128)(2,1)S(1)}, bf16[1152,1280]{1,0:T(8,128)(2,1)S(1)}, u32[]{:S(2)}, u32[]{:S(2)}) collective-permute-start(bf16[1152,1280]{1,0:T(8,128)(2,1)S(1)} %get-tuple-element.96.refs_8_.refs_9_.refs_4_), channel_id=1, source_target_pairs={{0,1},{1,0},{16,17},{17,16},{2,3},{3,2},{18,19},{19,18},{4,5},{5,4... | collective-permute-start | bytes 8847368 | tf_op jit(solution)/shard_map/ppermute | solution.py:56
  58.6 9.8 %collective-permute-start.20 = (bf16[640,1280]{1,0:T(8,128)(2,1)S(1)}, bf16[640,1280]{1,0:T(8,128)(2,1)S(1)}, u32[]{:S(2)}, u32[]{:S(2)}) collective-permute-start(bf16[640,1280]{1,0:T(8,128)(2,1)S(1)} %get-tuple-element.83), channel_id=1, source_target_pairs={{0,1},{1,0},{16,17},{17,16},{2,3},{3,2},{18,19},{19,18},{4,5},{5,4... | collective-permute-start | bytes 4915208 | tf_op jit(solution)/shard_map/ppermute | solution.py:56
  58.7 13.7 %collective-permute-start.17 = (bf16[640,1280]{1,0:T(8,128)(2,1)S(1)}, bf16[640,1280]{1,0:T(8,128)(2,1)S(1)}, u32[]{:S(2)}, u32[]{:S(2)}) collective-permute-start(bf16[640,1280]{1,0:T(8,128)(2,1)S(1)} %get-tuple-element.80), channel_id=1, source_target_pairs={{0,1},{1,0},{16,17},{17,16},{2,3},{3,2},{18,19},{19,18},{4,5},{5,4... | collective-permute-start | bytes 4915208 | tf_op jit(solution)/shard_map/ppermute | solution.py:56
  68.4 12.7 %collective-permute-start.22 = (bf16[144,1280]{1,0:T(8,128)(2,1)S(1)}, bf16[144,1280]{1,0:T(8,128)(2,1)S(1)}, u32[]{:S(2)}, u32[]{:S(2)}) collective-permute-start(bf16[144,1280]{1,0:T(8,128)(2,1)S(1)} %get-tuple-element.102), channel_id=1, source_target_pairs={{0,32},{1,33},{16,48},{17,49},{2,34},{3,35},{18,50},{19,51},{4,36}... | collective-permute-start | bytes 1105928 | tf_op jit(solution)/shard_map/ppermute | solution.py:56
  70.4 22.8 %collective-permute-start.32 = (bf16[160,1280]{1,0:T(8,128)(2,1)S(1)}, bf16[160,1280]{1,0:T(8,128)(2,1)S(1)}, u32[]{:S(2)}, u32[]{:S(2)}) collective-permute-start(bf16[160,1280]{1,0:T(8,128)(2,1)S(1)} %get-tuple-element.123), channel_id=1, source_target_pairs={{0,32},{1,33},{16,48},{17,49},{2,34},{3,35},{18,50},{19,51},{4,36}... | collective-permute-start | bytes 1228808 | tf_op jit(solution)/shard_map/ppermute | solution.py:56
  70.5 16.0 %collective-permute-start.33 = (bf16[160,1280]{1,0:T(8,128)(2,1)S(1)}, bf16[160,1280]{1,0:T(8,128)(2,1)S(1)}, u32[]{:S(2)}, u32[]{:S(2)}) collective-permute-start(bf16[160,1280]{1,0:T(8,128)(2,1)S(1)} %get-tuple-element.125), channel_id=1, source_target_pairs={{0,96},{1,97},{16,112},{17,113},{2,98},{3,99},{18,114},{19,115},{4... | collective-permute-start | bytes 1228808 | tf_op jit(solution)/shard_map/ppermute | solution.py:56
  81.2 25.5 %collective-permute-start.30 = (bf16[144,1280]{1,0:T(8,128)(2,1)S(1)}, bf16[144,1280]{1,0:T(8,128)(2,1)S(1)}, u32[]{:S(2)}, u32[]{:S(2)}) collective-permute-start(bf16[144,1280]{1,0:T(8,128)(2,1)S(1)} %add_rows.4), channel_id=1, source_target_pairs={{0,32},{1,33},{16,48},{17,49},{2,34},{3,35},{18,50},{19,51},{4,36}... | collective-permute-start | bytes 1105928 | tf_op jit(solution)/shard_map/ppermute | solution.py:56
  83.2 15.3 %collective-permute-start.23 = (bf16[160,1152]{1,0:T(8,128)(2,1)S(1)}, bf16[160,1152]{1,0:T(8,128)(2,1)S(1)}, u32[]{:S(2)}, u32[]{:S(2)}) collective-permute-start(bf16[160,1152]{1,0:T(8,128)(2,1)S(1)} %get-tuple-element.108), channel_id=1, source_target_pairs={{0,4},{1,5},{16,20},{17,21},{2,6},{3,7},{18,22},{19,23},{4,8},{5,9... | collective-permute-start | bytes 1105928 | tf_op jit(solution)/shard_map/ppermute | solution.py:56
  83.9 8.9 %collective-permute-start.26 = (bf16[160,1152]{1,0:T(8,128)(2,1)S(1)}, bf16[160,1152]{1,0:T(8,128)(2,1)S(1)}, u32[]{:S(2)}, u32[]{:S(2)}) collective-permute-start(bf16[160,1152]{1,0:T(8,128)(2,1)S(1)} %get-tuple-element.114), channel_id=1, source_target_pairs={{0,12},{1,13},{16,28},{17,29},{2,14},{3,15},{18,30},{19,31},{4,0},... | collective-permute-start | bytes 1105928 | tf_op jit(solution)/shard_map/ppermute | solution.py:56
  86.5 10.7 %collective-permute-start.34 = (bf16[160,1280]{1,0:T(8,128)(2,1)S(1)}, bf16[160,1280]{1,0:T(8,128)(2,1)S(1)}, u32[]{:S(2)}, u32[]{:S(2)}) collective-permute-start(bf16[160,1280]{1,0:T(8,128)(2,1)S(1)} %add_rows.7), channel_id=1, source_target_pairs={{0,96},{1,97},{16,112},{17,113},{2,98},{3,99},{18,114},{19,115},{4... | collective-permute-start | bytes 1228808 | tf_op jit(solution)/shard_map/ppermute | solution.py:56
  92.9 9.9 %collective-permute-start.27 = (bf16[160,1152]{1,0:T(8,128)(2,1)S(1)}, bf16[160,1152]{1,0:T(8,128)(2,1)S(1)}, u32[]{:S(2)}, u32[]{:S(2)}) collective-permute-start(bf16[160,1152]{1,0:T(8,128)(2,1)S(1)} %get-tuple-element.117), channel_id=1, source_target_pairs={{0,4},{1,5},{16,20},{17,21},{2,6},{3,7},{18,22},{19,23},{4,8},{5,9... | collective-permute-start | bytes 1105928 | tf_op jit(solution)/shard_map/ppermute | solution.py:56
  93.2 9.6 %collective-permute-start.28 = (bf16[160,1152]{1,0:T(8,128)(2,1)S(1)}, bf16[160,1152]{1,0:T(8,128)(2,1)S(1)}, u32[]{:S(2)}, u32[]{:S(2)}) collective-permute-start(bf16[160,1152]{1,0:T(8,128)(2,1)S(1)} %add_rows.6), channel_id=1, source_target_pairs={{0,12},{1,13},{16,28},{17,29},{2,14},{3,15},{18,30},{19,31},{4,0},... | collective-permute-start | bytes 1105928 | tf_op jit(solution)/shard_map/ppermute | solution.py:56
  97.4 11.5 %collective-permute-start.35 = (bf16[160,1280]{1,0:T(8,128)(2,1)S(1)}, bf16[160,1280]{1,0:T(8,128)(2,1)S(1)}, u32[]{:S(2)}, u32[]{:S(2)}) collective-permute-start(bf16[160,1280]{1,0:T(8,128)(2,1)S(1)} %add_three.3.gave), channel_id=1, source_target_pairs={{0,16},{1,17},{16,0},{17,1},{2,18},{3,19},{18,2},{19,3},{4,20},{5,... | collective-permute-start | bytes 1228808 | tf_op jit(solution)/shard_map/ppermute | solution.py:56
  98.6 10.3 %collective-permute-start.31 = (bf16[144,1280]{1,0:T(8,128)(2,1)S(1)}, bf16[144,1280]{1,0:T(8,128)(2,1)S(1)}, u32[]{:S(2)}, u32[]{:S(2)}) collective-permute-start(bf16[144,1280]{1,0:T(8,128)(2,1)S(1)} %get-tuple-element.121), channel_id=1, source_target_pairs={{0,96},{1,97},{16,112},{17,113},{2,98},{3,99},{18,114},{19,115},{4... | collective-permute-start | bytes 1105928 | tf_op jit(solution)/shard_map/ppermute | solution.py:56
  102.9 12.2 %collective-permute-start.29 = (bf16[160,1152]{1,0:T(8,128)(2,1)S(1)}, bf16[160,1152]{1,0:T(8,128)(2,1)S(1)}, u32[]{:S(2)}, u32[]{:S(2)}) collective-permute-start(bf16[160,1152]{1,0:T(8,128)(2,1)S(1)} %add_three.2), channel_id=1, source_target_pairs={{0,2},{1,3},{16,18},{17,19},{2,0},{3,1},{18,16},{19,17},{4,6},{5,7... | collective-permute-start | bytes 1105928 | tf_op jit(solution)/shard_map/ppermute | solution.py:56
  105.6 9.5 %collective-permute-start.24 = (bf16[160,1152]{1,0:T(8,128)(2,1)S(1)}, bf16[160,1152]{1,0:T(8,128)(2,1)S(1)}, u32[]{:S(2)}, u32[]{:S(2)}) collective-permute-start(bf16[160,1152]{1,0:T(8,128)(2,1)S(1)} %add_rows.5), channel_id=1, source_target_pairs={{0,4},{1,5},{16,20},{17,21},{2,6},{3,7},{18,22},{19,23},{4,8},{5,9... | collective-permute-start | bytes 1105928 | tf_op jit(solution)/shard_map/ppermute | solution.py:56
  106.7 8.4 %collective-permute-start.25 = (bf16[160,1152]{1,0:T(8,128)(2,1)S(1)}, bf16[160,1152]{1,0:T(8,128)(2,1)S(1)}, u32[]{:S(2)}, u32[]{:S(2)}) collective-permute-start(bf16[160,1152]{1,0:T(8,128)(2,1)S(1)} %get-tuple-element.111), channel_id=1, source_target_pairs={{0,12},{1,13},{16,28},{17,29},{2,14},{3,15},{18,30},{19,31},{4,0},... | collective-permute-start | bytes 1105928 | tf_op jit(solution)/shard_map/ppermute | solution.py:56
  (8 other events, 48.1 us)
